TPU v7x, 128 devices: a whole 4x4x4 slice. The times are simulated.
128 devices in a mesh: seq: 16 (over z, x), grp: 8 (over y, core).
Axes of the slice: x: 4, y: 4, z: 4, core: 2. Of those that a mesh axis runs over, the one named last changes fastest.
Arguments:
- query: bfloat16 [512, 24576], P(('grp', 'seq')), parts along dimension 0
- dec_query: bfloat16 [128, 24576], P(('grp', 'seq')), parts along dimension 0
- cache_kv: bfloat16 [131072, 576], P(('grp', 'seq')), parts along dimension 0
- span_kv: bfloat16 [512, 576], P(('grp', 'seq')), parts along dimension 0, may hold values from -4 to 4
- dec_kv: bfloat16 [128, 576], P(('grp', 'seq')), parts along dimension 0
- cache_fill: int32 [128], P('grp'), parts along dimension 0, may hold values from 128 to 960, as said below
- owner: int32 [512], P('grp'), parts along dimension 0, may hold values from 0 to 15, as said below
- slot: int32 [512], P('grp'), parts along dimension 0, may hold values from 128 to 1023, as said below
- dec_len: int32 [128], P('grp'), parts along dimension 0, may hold values from 1 to 64
- w_uk: bfloat16 [128, 128, 512], P('seq'), may hold values from -0.5 to 0.5
- w_uv: bfloat16 [128, 512, 128], P('seq'), may hold values from -0.25 to 0.25
Outputs:
- span_out: bfloat16 [512, 16384], P('grp', 'seq'), parts along dimension 0
- dec_out: bfloat16 [128, 16384], P('grp', 'seq'), parts along dimension 0
- new_cache: bfloat16 [131072, 576], P(('grp', 'seq')), parts along dimension 0
There are 8 independent parts, one for each index of `grp`. A program takes and returns all parts, laid end to end along the dimension named above; an argument that names none is the same for every part. Nothing has to cross between parts.
Inputs may be any that keep to these rules, and one draw needn't show every extreme that they name: `cache_fill`: every block keeps at least 128 filled slots and room for all 64 new rows. `owner`: a block index for each prefill token; blocks receive unequal numbers of rows. slot[t] = cache_fill[owner[t]] plus the number of earlier prefill tokens with the same owner.
All inputs are finite; a program needn't handle non-finite values.
Results may differ from a plain program's by a relative error of at most 0.014.
Values may be sent and summed in bfloat16 or wider, within the bound.
A program may use at most 192 MiB of HBM per device.

v0:
```python
import jax
import jax.numpy as jnp
from jax import lax
from jax.sharding import PartitionSpec as P

DN = 128
DC = 512


score_scale = 0.1353


def tag_rows(rows, cache_fill, owner, slot, pos_dev, span):
    block = rows // pos_dev
    local = rows % pos_dev
    count = cache_fill.shape[0]
    fills = jnp.sum(
        jnp.where(
            block[:, None] == jnp.arange(count, dtype=jnp.int32)[None, :], cache_fill[None, :], 0
        ),
        axis=1,
    )
    base = jnp.where(local < fills, -1, span + 1)
    target = owner * pos_dev + slot
    token = jnp.arange(span, dtype=jnp.int32)
    placed = jnp.sum(jnp.where(rows[:, None] == target[None, :], token[None, :] + 1, 0), axis=1)
    return jnp.where(placed > 0, placed - 1, base)


def combine(state, peak, total, output):
    old_peak, old_total, old_acc = state
    top = jnp.maximum(old_peak, peak)
    keep = jnp.exp(old_peak - top)
    fresh = jnp.exp(peak - top)
    return (
        top,
        old_total * keep + total * fresh,
        old_acc * keep[..., None] + output * fresh[..., None],
    )


def block_partial(absorbed, keys, tags, limits):
    scores = (
        jnp.einsum("qhc,pc->qhp", absorbed, keys, preferred_element_type=jnp.float32) * score_scale
    )
    visible = tags[None, None, :] < limits[:, None, None]
    peak = jnp.max(jnp.where(visible, scores, -1e30), axis=2)
    weights = jnp.where(visible, jnp.exp(scores - peak[..., None]), 0.0)
    total = jnp.sum(weights, axis=2)
    output = jnp.einsum(
        "qhp,pc->qhc",
        weights.astype(jnp.bfloat16),
        keys[:, :DC],
        preferred_element_type=jnp.float32,
    )
    return (peak, total, output)


def grouped(absorbed, keys, tags, limits):
    heads = absorbed.shape[1]
    group = 32
    count = heads // group
    rows = absorbed.shape[0]

    def one_group(index):
        return block_partial(
            lax.dynamic_slice_in_dim(absorbed, index * group, group, 1), keys, tags, limits
        )

    peak, total, output = lax.map(one_group, jnp.arange(count, dtype=jnp.int32))
    peak = jnp.moveaxis(peak, 0, 1).reshape(rows, heads)
    total = jnp.moveaxis(total, 0, 1).reshape(rows, heads)
    output = jnp.moveaxis(output, 0, 1).reshape(rows, heads, DC)
    return (peak, total, output)


def body(query, dec_query, cache_kv, span_kv, dec_kv, cache_fill, owner, slot, dec_len, w_uk, w_uv):
    me = lax.axis_index("seq")
    pos_dev = cache_kv.shape[0]
    span = owner.shape[0]
    new_rows, dec_keys = (
        lax.all_gather(span_kv, "seq", axis=0, tiled=True),
        lax.all_gather(dec_kv, "seq", axis=0, tiled=True),
    )
    local = jnp.arange(pos_dev, dtype=jnp.int32)
    target = jnp.where(owner == me, slot, -1)
    onehot = local[:, None] == target[None, :]
    placed = jnp.dot(
        onehot.astype(jnp.bfloat16), new_rows, preferred_element_type=jnp.float32
    ).astype(jnp.bfloat16)
    new_cache = jnp.where(jnp.any(onehot, axis=1)[:, None], placed, cache_kv)
    heads_all = w_uk.shape[0] * lax.axis_size("seq")
    width = query.shape[1] // heads_all
    q_span, q_dec = (
        lax.all_to_all(
            query.reshape(query.shape[0], heads_all, width),
            "seq",
            split_axis=1,
            concat_axis=0,
            tiled=True,
        ),
        lax.all_to_all(
            dec_query.reshape(dec_query.shape[0], heads_all, width),
            "seq",
            split_axis=1,
            concat_axis=0,
            tiled=True,
        ),
    )
    both = jnp.concatenate([q_span, q_dec], axis=0)
    latent = jnp.einsum(
        "thn,hnc->thc", both[:, :, :DN], w_uk, preferred_element_type=jnp.float32
    ).astype(jnp.bfloat16)
    absorbed = jnp.concatenate([latent, both[:, :, DN:]], axis=2)
    limits = jnp.concatenate([jnp.arange(1, span + 1, dtype=jnp.int32), dec_len])
    count = absorbed.shape[0]
    heads = absorbed.shape[1]
    everyone = lax.all_gather(absorbed, "seq", axis=1, tiled=True)
    rows = me * pos_dev + local
    peak, total, output = grouped(
        everyone, new_cache, tag_rows(rows, cache_fill, owner, slot, pos_dev, span), limits
    )
    peaks, totals, outputs = (
        lax.all_to_all(peak[None], "seq", split_axis=2, concat_axis=0, tiled=True),
        lax.all_to_all(total[None], "seq", split_axis=2, concat_axis=0, tiled=True),
        lax.all_to_all(output[None], "seq", split_axis=2, concat_axis=0, tiled=True),
    )
    peak = jnp.max(peaks, axis=0)
    factor = jnp.exp(peaks - peak[None])
    total = jnp.sum(factor * totals, axis=0)
    acc = jnp.sum(factor[..., None] * outputs, axis=0)
    dec_abs = absorbed[span:]
    own = (
        jnp.einsum("rhc,rc->rh", dec_abs, dec_keys, preferred_element_type=jnp.float32)
        * score_scale
    )
    rows_dec = dec_abs.shape[0]
    own_out = jnp.broadcast_to(dec_keys[:, None, :DC].astype(jnp.float32), (rows_dec, heads, DC))
    dec_state = combine(
        (peak[span:], total[span:], acc[span:]),
        own,
        jnp.ones((rows_dec, heads), jnp.float32),
        own_out,
    )
    total = jnp.concatenate([total[:span], dec_state[1]], axis=0)
    acc = jnp.concatenate([acc[:span], dec_state[2]], axis=0)
    latent_out = (acc / total[..., None]).astype(jnp.bfloat16)
    result = jnp.einsum(
        "qhc,hcv->qhv", latent_out, w_uv, preferred_element_type=jnp.float32
    ).astype(jnp.bfloat16)
    result = result.reshape(count, heads * w_uv.shape[2])
    return (result[:span], result[span:], new_cache)


def solution(mesh):
    in_specs = (
        P(("grp", "seq"), None),
        P(("grp", "seq"), None),
        P(("grp", "seq"), None),
        P(("grp", "seq"), None),
        P(("grp", "seq"), None),
        P("grp"),
        P("grp"),
        P("grp"),
        P("grp"),
        P("seq", None, None),
        P("seq", None, None),
    )
    out_specs = (P("grp", "seq"), P("grp", "seq"), P(("grp", "seq"), None))
    return jax.shard_map(body, mesh=mesh, in_specs=in_specs, out_specs=out_specs, check_vma=False)
```

profile of v0, /device:TPU:0, one launch (start us, length us, event | category | flops | bytes accessed | tf_op | source)
XLA Modules:
  0.0 597.5 jit_solution(13242310837493840628)
XLA Ops:
  7.2 1.2 reduce.1
  8.6 0.5 broadcast.100
  9.1 1.0 reduce.2
  10.1 0.7 reshape.104
  10.9 8.0 %all-to-all-start.1 = ((bf16[16,2,768]{2,1,0:T(2,128)(2,1)}), bf16[16,2,768]{2,1,0:T(2,128)(2,1)S(1)}, u32[]{:S(2)}, u32[]{:S(2)}) async-start(bf16[16,2,768]{2,1,0:T(2,128)(2,1)} %reshape.104), calls=%async_computation.1 | async-start | bytes 98304 | tf_op jit(solution)/shard_map/all_to_all | solution.py:102
  18.8 1.2 reshape.91
  20.1 0.9 copy.93
  21.0 5.5 all-to-all-done.1
  26.5 3.5 all-to-all-start
  30.2 8.5 %all-to-all-done = bf16[4,128,192]{2,0,1:T(4,128)(2,1)S(1)} async-done(((bf16[4,128,192]{2,0,1:T(4,128)(2,1)}), bf16[4,128,192]{2,0,1:T(4,128)(2,1)S(1)}, u32[]{:S(2)}, u32[]{:S(2)}) %all-to-all-start) | async-done | bytes 196640 | tf_op jit(solution)/shard_map/all_to_all | solution.py:95
  39.5 1.0 pad_maximum_fusion
  40.5 21.7 %all-gather = bf16[16,4,576]{2,1,0:T(4,128)(2,1)S(1)} all-gather(bf16[1,4,576]{2,1,0:T(4,128)(2,1)} %bitcast.114), channel_id=1, replica_groups=mesh['seq'=16,'grp'=8] {'seq'}, dimensions={0}, use_global_device_ids=true | all-gather | bytes 78336 | tf_op jit(solution)/shard_map/all_gather | solution.py:82
  62.3 0.7 compare_select_fusion
  63.1 1.8 fusion.18
  65.0 1.5 copy.99
  66.7 64.5 %all-gather.4.cloned.1.call-done = bf16[80,128,576]{2,0,1:T(8,128)(2,1)} async-done(((bf16[80,8,576]{2,0,1:T(8,128)(2,1)}), bf16[80,128,576]{2,0,1:T(8,128)(2,1)}) %all-gather.4.cloned.1.call-update) | async-done | bytes 11796496 | tf_op jit(solution)/shard_map/all_gather | solution.py:118
  131.2 72.5 %while.14 = (s32[]{:T(128)}, f32[4,80,32]{2,1,0:T(8,128)S(1)}, f32[4,80,32]{2,1,0:T(8,128)S(1)}, f32[4,80,32,512]{3,2,0,1:T(8,128)}, s32[1024]{0:T(1024)S(1)}, /...) while((s32[]{:T(128)}, f32[4,80,32]{2,1,0:T(8,128)S(1)}, ...), condition=%wide.region_6.7_spmd, body=%wide.region_3.6_spmd.sunk | while | flops 5733166080 | bytes 53062180 | solution.py:70
  131.2 0.6 dynamic_slice.11
  132.6 2.2 constant_dynamic-slice_fusion.2
  134.8 6.5 %select_reduce_fusion.4 = (f32[80,32]{1,0:T(8,128)S(1)}, f32[80,32,1024]{2,1,0:T(8,128)S(1)}) fusion(pred[80,1024]{1,0:T(8,128)(4,1)S(1)} %broadcast_compare_fusion.2, bf16[1024,576]{1,0:T(8,128)(2,1)} %get-tuple-element.237, bf16[80,32,576]{2,0,1:T(8,128)(2,1)S(1)} %constant_dynamic-slice_fusion.2), kind=kOutput, calls=%fused_computation.1.clone.1 | convolution fusion | flops 3027760640 | bytes 14706688 | tf_op jit(solution)/shard_map/while/body/eval_jaxpr/qhc,pc->qhp/dot_general | solution.py:44
  141.3 3.1 fusion.49
  144.5 4.9 bitcast_dynamic-update-slice_fusion.6
  149.3 0.6 dynamic_slice.11
  150.7 2.2 constant_dynamic-slice_fusion.2
  152.9 6.5 %select_reduce_fusion.4 = (f32[80,32]{1,0:T(8,128)S(1)}, f32[80,32,1024]{2,1,0:T(8,128)S(1)}) fusion(pred[80,1024]{1,0:T(8,128)(4,1)S(1)} %broadcast_compare_fusion.2, bf16[1024,576]{1,0:T(8,128)(2,1)} %get-tuple-element.237, bf16[80,32,576]{2,0,1:T(8,128)(2,1)S(1)} %constant_dynamic-slice_fusion.2), kind=kOutput, calls=%fused_computation.1.clone.1 | convolution fusion | flops 3027760640 | bytes 14706688 | tf_op jit(solution)/shard_map/while/body/eval_jaxpr/qhc,pc->qhp/dot_general | solution.py:44
  159.4 3.1 fusion.49
  162.6 4.9 bitcast_dynamic-update-slice_fusion.6
  167.5 0.6 dynamic_slice.11
  168.8 2.2 constant_dynamic-slice_fusion.2
  171.0 6.5 %select_reduce_fusion.4 = (f32[80,32]{1,0:T(8,128)S(1)}, f32[80,32,1024]{2,1,0:T(8,128)S(1)}) fusion(pred[80,1024]{1,0:T(8,128)(4,1)S(1)} %broadcast_compare_fusion.2, bf16[1024,576]{1,0:T(8,128)(2,1)} %get-tuple-element.237, bf16[80,32,576]{2,0,1:T(8,128)(2,1)S(1)} %constant_dynamic-slice_fusion.2), kind=kOutput, calls=%fused_computation.1.clone.1 | convolution fusion | flops 3027760640 | bytes 14706688 | tf_op jit(solution)/shard_map/while/body/eval_jaxpr/qhc,pc->qhp/dot_general | solution.py:44
  177.5 3.1 fusion.49
  180.7 4.9 bitcast_dynamic-update-slice_fusion.6
  185.6 0.6 dynamic_slice.11
  186.9 2.2 constant_dynamic-slice_fusion.2
  189.2 6.5 %select_reduce_fusion.4 = (f32[80,32]{1,0:T(8,128)S(1)}, f32[80,32,1024]{2,1,0:T(8,128)S(1)}) fusion(pred[80,1024]{1,0:T(8,128)(4,1)S(1)} %broadcast_compare_fusion.2, bf16[1024,576]{1,0:T(8,128)(2,1)} %get-tuple-element.237, bf16[80,32,576]{2,0,1:T(8,128)(2,1)S(1)} %constant_dynamic-slice_fusion.2), kind=kOutput, calls=%fused_computation.1.clone.1 | convolution fusion | flops 3027760640 | bytes 14706688 | tf_op jit(solution)/shard_map/while/body/eval_jaxpr/qhc,pc->qhp/dot_general | solution.py:44
  195.7 3.1 fusion.49
  198.8 4.9 bitcast_dynamic-update-slice_fusion.6
  203.7 0.7 copy.100
  204.4 5.2 all-to-all-start.2
  209.7 0.7 copy.108
  210.4 6.9 %all-to-all-done.2 = f32[1,80,128]{1,0,2:T(1,128)S(1)} async-done(((f32[1,80,128]{1,0,2:T(1,128)}), f32[1,80,128]{1,0,2:T(1,128)S(1)}, u32[]{:S(2)}, u32[]{:S(2)}) %all-to-all-start.2) | async-done | bytes 40992 | tf_op jit(solution)/shard_map/all_to_all | solution.py:124
  217.3 3.7 all-to-all-start.4
  221.1 21.3 %copy.104 = f32[1,80,128,512]{3,1,0,2:T(8,128)} copy(f32[1,80,128,512]{3,2,1,0:T(8,128)} %bitcast.102) | data formatting | bytes 41943040 | tf_op jit(solution)/shard_map/broadcast_in_dim;reshape | solution.py:126
  242.4 7.1 %all-to-all-start.3 = ((f32[1,80,128,512]{3,1,0,2:T(8,128)}), f32[1,80,128,512]{3,1,0,2:T(8,128)}, u32[]{:S(2)}, u32[]{:S(2)}) async-start(f32[1,80,128,512]{3,1,0,2:T(8,128)} %copy.104), calls=%async_computation.3 | async-start | bytes 41943040 | tf_op jit(solution)/shard_map/all_to_all | solution.py:126
  249.5 318.8 %all-gather.1 = bf16[16,1,576]{2,1,0:T(2,128)(2,1)S(1)} all-gather(bf16[1,1,576]{2,1,0:T(2,128)(2,1)S(1)} %bitcast.115), channel_id=1, replica_groups=mesh['seq'=16,'grp'=8] {'seq'}, dimensions={0}, use_global_device_ids=true | all-gather | bytes 19584 | tf_op jit(solution)/shard_map/all_gather | solution.py:83
  569.5 19.0 %fusion.17 = f32[80,8,512]{2,1,0:T(8,128)S(1)} fusion(f32[1,80,128,512]{3,1,0,2:T(8,128)} %all-to-all-done.3, f32[16,80,8]{2,0,1:T(8,128)S(1)} %copy.102), kind=kLoop, calls=%fused_computation.22 | loop fusion | flops 10158080 | bytes 22323200 | tf_op jit(solution)/shard_map/reduce_sum | solution.py:131
  589.4 0.6 copy_bitcast_fusion.3
  590.0 0.7 copy_bitcast_fusion.1
  (73 shorter events, 4.1 us)
Async XLA Ops:
  7.2 32.0 %copy-start = (bf16[8,128,512]{2,1,0:T(8,128)(2,1)S(1)}, bf16[8,128,512]{2,1,0:T(8,128)(2,1)}, u32[]{:S(2)}) copy-start(bf16[8,128,512]{2,1,0:T(8,128)(2,1)} %param.22) | copy-start | bytes 3145732
  7.2 59.2 %copy-start.7 = (s32[16]{0:T(128)S(1)}, s32[16]{0:T(128)}, u32[]{:S(2)}) copy-start(s32[16]{0:T(128)} %param.21) | copy-start | bytes 196
  7.2 59.3 %copy-start.6 = (s32[16]{0:T(128)S(1)}, s32[16]{0:T(128)}, u32[]{:S(2)}) copy-start(s32[16]{0:T(128)} %param.18) | copy-start | bytes 196
  10.9 15.6 %all-to-all-start.1 = ((bf16[16,2,768]{2,1,0:T(2,128)(2,1)}), bf16[16,2,768]{2,1,0:T(2,128)(2,1)S(1)}, u32[]{:S(2)}, u32[]{:S(2)}) async-start(bf16[16,2,768]{2,1,0:T(2,128)(2,1)} %reshape.104), calls=%async_computation.1 | async-start | bytes 98304 | tf_op jit(solution)/shard_map/all_to_all | solution.py:102
  26.5 12.2 %all-to-all-start = ((bf16[4,128,192]{2,0,1:T(4,128)(2,1)}), bf16[4,128,192]{2,0,1:T(4,128)(2,1)S(1)}, u32[]{:S(2)}, u32[]{:S(2)}) async-start(bf16[4,128,192]{2,0,1:T(4,128)(2,1)} %copy.93), calls=%async_computation | async-start | bytes 524288 | tf_op jit(solution)/shard_map/all_to_all | solution.py:95
  30.0 101.2 %all-gather.4.cloned.1.call-start = ((), (), s32[]{:S(2)}) async-start(), calls=%async_computation.5 | async-start | bytes 13926400 | tf_op jit(solution)/shard_map/all_gather | solution.py:118
  64.9 66.3 %copy-start.2 = (bf16[1024,576]{0,1:T(8,128)(2,1)}, bf16[1024,576]{0,1:T(8,128)(2,1)S(1)}, u32[]{:S(2)}) copy-start(bf16[1024,576]{0,1:T(8,128)(2,1)S(1)} %fusion.18) | copy-start | bytes 3538948
  141.3 3.1 copy-start.3
  159.4 3.1 copy-start.3
  177.5 3.1 copy-start.3
  195.6 3.1 copy-start.3
  204.4 12.9 %all-to-all-start.2 = ((f32[1,80,128]{1,0,2:T(1,128)}), f32[1,80,128]{1,0,2:T(1,128)S(1)}, u32[]{:S(2)}, u32[]{:S(2)}) async-start(f32[1,80,128]{1,0,2:T(1,128)} %bitcast.12), calls=%async_computation.2 | async-start | bytes 131072 | tf_op jit(solution)/shard_map/all_to_all | solution.py:124
  217.3 25.1 %all-to-all-start.4 = ((f32[1,80,128]{1,0,2:T(1,128)}), f32[1,80,128]{1,0,2:T(1,128)S(1)}, u32[]{:S(2)}, u32[]{:S(2)}) async-start(f32[1,80,128]{1,0,2:T(1,128)} %bitcast.27), calls=%async_computation.4 | async-start | bytes 131072 | tf_op jit(solution)/shard_map/all_to_all | solution.py:125
  242.4 7.1 %copy-start.5 = (bf16[1,576]{1,0:T(2,128)(2,1)S(1)}, bf16[1,576]{1,0:T(2,128)(2,1)}, u32[]{:S(2)}) copy-start(bf16[1,576]{1,0:T(2,128)(2,1)} %param.17) | copy-start | bytes 3460
  242.4 327.1 %all-to-all-start.3 = ((f32[1,80,128,512]{3,1,0,2:T(8,128)}), f32[1,80,128,512]{3,1,0,2:T(8,128)}, u32[]{:S(2)}, u32[]{:S(2)}) async-start(f32[1,80,128,512]{3,1,0,2:T(8,128)} %copy.104), calls=%async_computation.3 | async-start | bytes 41943040 | tf_op jit(solution)/shard_map/all_to_all | solution.py:126
  569.1 21.6 %copy-start.1 = (bf16[8,128,512]{2,1,0:T(8,128)(2,1)S(1)}, bf16[8,128,512]{2,1,0:T(8,128)(2,1)}, u32[]{:S(2)}) copy-start(bf16[8,128,512]{2,1,0:T(8,128)(2,1)} %param.22) | copy-start | bytes 3145732
  569.5 19.4 %copy-start.4 = (bf16[8,512,128]{2,1,0:T(8,128)(2,1)S(1)}, bf16[8,512,128]{2,1,0:T(8,128)(2,1)}, u32[]{:S(2)}) copy-start(bf16[8,512,128]{2,1,0:T(8,128)(2,1)} %param.23) | copy-start | bytes 3145732
Sparse Core Ops, SparseCore 0:
  40.6 90.5 all-gather.3
where the time goes:
time: 599 us; the launch traced here: 598 us
  blocking collectives  341 us (57%)
  waiting for transfers between devices  85.4 us (14%)
  matrix products  48.4 us (8%)
  local copies, waits for them, and re-layouts  41.7 us (7%)
  other arithmetic  36.8 us (6%)
  starting transfers between devices  27.6 us (5%)
  between operations  14.4 us (2%)
    all_gather x1, blocking collectives, body(): lax.all_gather(dec_kv, 'seq', axis=0, tiled=True)  319 us
    all_gather x1, waiting for transfers between devices, body(): everyone = lax.all_gather(absorbed, 'seq', axis=1, tiled=True)  64.5 us
    dot_general x4, matrix products, block_partial(): jnp.einsum('qhc,pc->qhp', absorbed, keys, preferred_element_type=jnp.floa...  26 us
    all_gather x1, blocking collectives, body(): lax.all_gather(span_kv, 'seq', axis=0, tiled=True)  21.7 us
    another operation x1, local copies, waits for them, and re-layouts, body(): output[None]  21.3 us
    dot_general x4, matrix products, block_partial(): jnp.einsum('qhp,pc->qhc', weights.astype(jnp.bfloat16), keys[:, :DC], pre...  19.6 us
    reduce_sum x1, other arithmetic, body(): acc = jnp.sum(factor[..., None] * outputs, axis=0)  19 us
    reduce_sum x4, other arithmetic, block_partial(): total = jnp.sum(weights, axis=2)  12.4 us
  transfers between devices with their start and end apart: 6, of which 4 were waited for; matrix products, arithmetic and copies ran while one was open for 5% of the time, Pallas kernels for 0%

commit v1 on v0

v1 whole, which is shorter than its diff:
```python
import functools
import math

import jax
import jax.numpy as jnp
from jax import lax
from jax.experimental import pallas as pl
from jax.experimental.pallas import tpu as pltpu
from jax.sharding import PartitionSpec as P

MESH = pl.DeviceIdType.MESH
F32 = jnp.float32
BF16 = jnp.bfloat16

SIDE = 4
SEQ = SIDE * SIDE
HEADS = 8
DN = 128
DR = 64
DC = 512
DV = 128
WIDE = DC + 128
POS = 1024
SPAN = 64
ROWS = 16
COUNT = SPAN + ROWS
QROWS = HEADS * COUNT
SLICE = HEADS * (DN + DR)
TILE = 320
CHUNK = 256

SCALE2 = 0.1353 * math.log2(math.e)
LOW = -1e30


def dot(a, b):
    return jnp.dot(a, b, preferred_element_type=F32)


def dot_t(a, b):
    return lax.dot_general(a, b, (((1,), (1,)), ((), ())), preferred_element_type=F32)


def lane_mask(shape):
    return lax.broadcasted_iota(jnp.int32, shape, len(shape) - 1) < DR


def doubled(first):
    row = lax.broadcasted_iota(jnp.int32, (128, 128), 0)
    col = lax.broadcasted_iota(jnp.int32, (128, 128), 1)
    want = lax.rem(col, DR) + (0 if first else DR)
    return jnp.where(row == want, 1.0, 0.0).astype(BF16)


def kernel(
    q_ref, kv_ref, cache_ref, fill_ref, owner_ref, slot_ref, dlen_ref, uk_ref, uv_ref,
    span_ref, dec_ref, newc_ref,
    qbuf, kvbuf, q_all, qr_all, k_all, kr_all, k_own, acc, peak, total, score,
    o_send, e_send, o_recv, e_recv,
    local_sem, a_send, a_recv, c_send, c_recv, h_send, h_recv, p_send, p_recv,
):
    seq, grp = lax.axis_index("seq"), lax.axis_index("grp")
    core = lax.rem(grp, 2)
    z, x = seq // SIDE, lax.rem(seq, SIDE)

    def along_z(d):
        return lax.rem(z + d + SIDE, SIDE) * SIDE + x

    def along_x(d):
        return z * SIDE + lax.rem(x + d + SIDE, SIDE)

    def cache_peer(d):
        return (1 - core) * along_z(d) + core * along_x(d)

    def head_peer(d):
        return core * along_z(d) + (1 - core) * along_x(d)

    def remote(src, dst, send, recv, peer):
        return pltpu.make_async_remote_copy(
            src_ref=src, dst_ref=dst, send_sem=send, recv_sem=recv,
            device_id=(peer, grp), device_id_type=MESH,
        )

    barrier = pltpu.get_barrier_semaphore()
    for d in range(1, SEQ):
        pl.semaphore_signal(
            barrier, inc=1, device_id=(lax.rem(seq + d, SEQ), grp), device_id_type=MESH
        )

    own_q = pltpu.make_async_copy(
        q_ref.at[:, pl.ds(pl.multiple_of(seq * SLICE, 128), SLICE)], qbuf.at[seq], local_sem.at[0]
    )
    own_kv = pltpu.make_async_copy(kv_ref, kvbuf.at[seq], local_sem.at[1])
    own_q.start()
    own_kv.start()

    row = lax.broadcasted_iota(jnp.int32, (DR, 128), 0)
    col = lax.broadcasted_iota(jnp.int32, (DR, 128), 1)
    left = jnp.where(row == col, 1.0, 0.0).astype(BF16)
    right = jnp.where(row + DR == col, 1.0, 0.0).astype(BF16)
    rope_lo = cache_ref[0 : POS // 2, DC : DC + DR]
    rope_hi = cache_ref[POS // 2 : POS, DC : DC + DR]
    kr_all[0] = (dot(rope_lo, left) + dot(rope_hi, right)).astype(BF16)

    pl.semaphore_wait(barrier, SEQ - 1)

    exchange = []
    for d in range(1, SEQ):
        peer = lax.rem(seq + d, SEQ)
        exchange.append(
            remote(
                q_ref.at[:, pl.ds(pl.multiple_of(peer * SLICE, 128), SLICE)],
                qbuf.at[seq], a_send.at[d - 1], a_recv.at[d - 1], peer,
            )
        )
        exchange.append(
            remote(kv_ref, kvbuf.at[seq], a_send.at[SEQ + d - 2], a_recv.at[SEQ + d - 2], peer)
        )
    for c in exchange:
        c.start()

    def part(ref, slot, lo, n, width):
        return ref.at[slot, pl.ds(lo, n), pl.ds(0, width)]

    def ring(whole, packed, own, send, recv, peer_of, rows, packs):
        half, pack = rows // 2, packs // 2

        def pair(i, src_slot, dst_slot, h, peer):
            src = own.at[pl.ds(h * half, half), pl.ds(0, DC)]
            if src_slot:
                src = part(whole, src_slot, h * half, half, DC)
            return [
                remote(src, part(whole, dst_slot, h * half, half, DC), send.at[2 * i], recv.at[2 * i], peer),
                remote(
                    packed.at[src_slot, pl.ds(h * pack, pack)], packed.at[dst_slot, pl.ds(h * pack, pack)],
                    send.at[2 * i + 1], recv.at[2 * i + 1], peer,
                ),
            ]

        up, down = peer_of(1), peer_of(-1)
        first_up = pair(0, 0, 1, 0, up)
        first_down = pair(1, 0, 3, 1, down)
        second_up = pair(2, 0, 1, 1, up)
        second_down = pair(3, 0, 3, 0, down)
        onward_up = pair(4, 1, 2, 0, up)
        onward_down = pair(5, 3, 2, 1, down)
        return first_up, first_down, second_up, second_down, onward_up, onward_down

    def start(*groups):
        for g in groups:
            for c in g:
                c.start()

    def arrived(*groups):
        for g in groups:
            for c in g:
                c.wait_recv()

    def sent(*groups):
        for g in groups:
            for c in g:
                c.wait_send()

    cring = ring(k_all, kr_all, cache_ref, c_send, c_recv, cache_peer, POS, POS // 2)
    start(*cring[:4])

    lo2, hi2 = doubled(True), doubled(False)

    def unpack_keys(slot):
        k_all[slot, 0 : POS // 2, DC:WIDE] = dot(kr_all[slot], lo2).astype(BF16)
        k_all[slot, POS // 2 : POS, DC:WIDE] = dot(kr_all[slot], hi2).astype(BF16)

    def unpack_queries(slot):
        for p in range(HEADS // 2):
            both = qr_all[slot, COUNT * p : COUNT * (p + 1), :].astype(F32)
            mask = lane_mask(both.shape)
            at = 2 * COUNT * p
            q_all[slot, at : at + COUNT, DC:WIDE] = jnp.where(mask, both, 0.0).astype(BF16)
            q_all[slot, at + COUNT : at + 2 * COUNT, DC:WIDE] = jnp.where(mask, 0.0, both).astype(BF16)

    k_all[0, :, 0:DC] = cache_ref[:, 0:DC]
    unpack_keys(0)
    peak[...] = jnp.full(peak.shape, LOW, F32)
    total[...] = jnp.zeros(total.shape, F32)
    acc[...] = jnp.zeros(acc.shape, F32)

    own_q.wait()
    own_kv.wait()
    for c in exchange:
        c.wait_recv()
    prow = lax.broadcasted_iota(jnp.int32, (COUNT, 128), 0)
    pcol = lax.broadcasted_iota(jnp.int32, (COUNT, 128), 1)
    place = jnp.where(prow < SPAN, 8 * (prow // 4) + lax.rem(prow, 4), 8 * (prow - SPAN) + 4)
    order = jnp.where(pcol == place, 1.0, 0.0).astype(BF16)
    q_rows = qbuf[...].astype(F32).reshape(8 * SEQ, SLICE).astype(BF16)
    q_rows = dot(order, q_rows)
    for p in range(HEADS // 2):
        at = 3 * 128 * p
        t0, t1, t2 = (q_rows[:, at + 128 * i : at + 128 * (i + 1)] for i in range(3))
        mask = lane_mask(t0.shape)
        nope = t0.astype(BF16)
        swapped = jnp.where(mask, t2, t1).astype(BF16)
        qr_all[0, COUNT * p : COUNT * (p + 1), :] = jnp.where(mask, t1, t2).astype(BF16)
        weight = uk_ref[2 * p + 1]
        weight = jnp.concatenate([weight[DR:], weight[:DR]], axis=0)
        row0 = 2 * COUNT * p
        q_all[0, row0 : row0 + COUNT, 0:DC] = dot(nope, uk_ref[2 * p]).astype(BF16)
        q_all[0, row0 + COUNT : row0 + 2 * COUNT, 0:DC] = dot(swapped, weight).astype(BF16)

    hring = ring(q_all, qr_all, q_all.at[0], h_send, h_recv, head_peer, QROWS, QROWS // 2)
    start(*hring[:4])
    unpack_queries(0)

    kv_rows = kvbuf[...].astype(F32).reshape(8 * SEQ, WIDE).astype(BF16)
    kv_rows = dot(order, kv_rows).astype(BF16)
    k_own[...] = jnp.zeros(k_own.shape, BF16)
    k_own[0:COUNT, 0:DC] = kv_rows[:, 0:DC]
    k_own[0:COUNT, DC:WIDE] = dot(kv_rows[:, DC:WIDE], lo2).astype(BF16)

    target = jnp.where(owner_ref[...] == seq, slot_ref[...], -1)
    span_rows = kv_rows[0:SPAN, 0 : DC + DR]

    @pl.loop(0, POS // 128)
    def _(i):
        at = pl.multiple_of(i * 128, 128)
        local = lax.broadcasted_iota(jnp.int32, (128, SPAN), 0) + at
        hot = jnp.where(local == target, 1.0, 0.0)
        put = dot(hot.astype(BF16), span_rows)
        any_hot = jnp.sum(hot, axis=1, keepdims=True) > 0.0
        old = cache_ref[pl.ds(at, 128), :].astype(F32)
        newc_ref[pl.ds(at, 128), :] = jnp.where(any_hot, put, old).astype(BF16)

    def attend(hs, ks):
        fill = fill_ref[cache_peer_back(ks)]

        @pl.loop(0, QROWS // TILE)
        def _(t):
            rows = pl.ds(pl.multiple_of(t * TILE, TILE), TILE)
            queries = q_all[hs, rows, :]
            top = peak[hs, rows, :]
            old = top
            for j in range(POS // CHUNK):
                s = dot_t(queries, k_all[ks, j * CHUNK : (j + 1) * CHUNK, :])
                at = lax.broadcasted_iota(jnp.int32, (1, CHUNK), 1) + j * CHUNK
                s = jnp.where(at < fill, s, LOW)
                score[:, j * CHUNK : (j + 1) * CHUNK] = s
                top = jnp.maximum(top, jnp.max(s, axis=1, keepdims=True))
            keep = jnp.exp2((old - top) * SCALE2)
            out = jnp.zeros((TILE, DC), F32)
            add = jnp.zeros((TILE, 1), F32)
            for j in range(POS // CHUNK):
                e = jnp.exp2((score[:, j * CHUNK : (j + 1) * CHUNK] - top) * SCALE2)
                add += jnp.sum(e, axis=1, keepdims=True)
                out += dot(e.astype(BF16), k_all[ks, j * CHUNK : (j + 1) * CHUNK, 0:DC])
            peak[hs, rows, :] = top
            total[hs, rows, :] = total[hs, rows, :] * keep + add
            acc[hs, rows, :] = acc[hs, rows, :] * keep + out

    def cache_peer_back(ks):
        return cache_peer(-ks)

    eye = lax.broadcasted_iota(jnp.int32, (128, 128), 0) == lax.broadcasted_iota(
        jnp.int32, (128, 128), 1
    )

    def finish(hs):
        t = total[hs]
        o_send[hs - 1] = (acc[hs] * (1.0 / t)).astype(BF16)
        level = peak[hs] * SCALE2 + jnp.log2(t)
        for i in range(QROWS // 128):
            square = jnp.broadcast_to(level[128 * i : 128 * (i + 1)], (128, 128))
            e_send[hs - 1, i : i + 1, :] = jnp.sum(jnp.where(eye, square, 0.0), axis=0, keepdims=True)

    def back(hs):
        peer = head_peer(-hs)
        return [
            remote(o_send.at[hs - 1], o_recv.at[hs - 1], p_send.at[2 * hs - 2], p_recv.at[2 * hs - 2], peer),
            remote(e_send.at[hs - 1], e_recv.at[hs - 1], p_send.at[2 * hs - 1], p_recv.at[2 * hs - 1], peer),
        ]

    e_send[...] = jnp.zeros(e_send.shape, F32)
    attend(0, 0)

    qrow = lax.broadcasted_iota(jnp.int32, (COUNT, 128), 0)
    kcol = lax.broadcasted_iota(jnp.int32, (COUNT, 128), 1)
    limit = jnp.where(qrow < SPAN, qrow + 1, 0)
    for r in range(ROWS):
        limit = jnp.where(qrow == SPAN + r, dlen_ref[r], limit)
    seen = (kcol < limit) | ((qrow >= SPAN) & (kcol == qrow))
    for h in range(HEADS):
        rows = slice(COUNT * h, COUNT * (h + 1))
        s = jnp.where(seen, dot_t(q_all[0, rows, :], k_own[...]), LOW)
        old = peak[0, rows, :]
        top = jnp.maximum(old, jnp.max(s, axis=1, keepdims=True))
        keep = jnp.exp2((old - top) * SCALE2)
        e = jnp.exp2((s - top) * SCALE2)
        peak[0, rows, :] = top
        total[0, rows, :] = total[0, rows, :] * keep + jnp.sum(e, axis=1, keepdims=True)
        acc[0, rows, :] = acc[0, rows, :] * keep + dot(e.astype(BF16), k_own[:, 0:DC])

    arrived(hring[0], hring[1])
    start(hring[4], hring[5])
    arrived(hring[2], hring[3])
    unpack_queries(1)
    unpack_queries(3)

    @pl.loop(0, 2)
    def _(i):
        attend(1 + 2 * i, 0)

    arrived(cring[0], cring[1])
    start(cring[4], cring[5])
    arrived(cring[2], cring[3])
    unpack_keys(1)
    unpack_keys(3)

    @pl.loop(0, 6)
    def _(i):
        j = lax.rem(i, 3)
        attend(j + j // 2, 1 + 2 * (i // 3))

    arrived(hring[4], hring[5])
    unpack_queries(2)

    @pl.loop(0, 3)
    def _(i):
        attend(2, i + i // 2)

    arrived(cring[4], cring[5])
    unpack_keys(2)

    @pl.loop(0, 3)
    def _(i):
        hs = 2 - i + 3 * (i // 2)
        attend(hs, 2)
        finish(hs)
        start(back(hs))

    attend(0, 2)

    own_level = peak[0] * SCALE2 + jnp.log2(total[0])
    levels = []
    for hs in range(1, SIDE):
        arrived(back(hs))
        column = []
        for i in range(QROWS // 128):
            square = jnp.broadcast_to(e_recv[hs - 1, i : i + 1, :], (128, 128))
            column.append(jnp.sum(jnp.where(eye, square, 0.0), axis=1, keepdims=True))
        levels.append(jnp.concatenate(column, axis=0))
    top = own_level
    for level in levels:
        top = jnp.maximum(top, level)
    weight = jnp.exp2(own_level - top)
    norm = weight
    shares = []
    for level in levels:
        share = jnp.exp2(level - top)
        shares.append(share)
        norm = norm + share
    norm = 1.0 / norm
    first = weight * norm / total[0]
    shares = [share * norm for share in shares]
    for h in range(HEADS):
        rows = slice(COUNT * h, COUNT * (h + 1))
        latent = acc[0, rows, :] * first[rows]
        for i in range(SIDE - 1):
            latent = latent + o_recv[i, rows, :].astype(F32) * shares[i][rows]
        value = dot(latent.astype(BF16), uv_ref[h]).astype(BF16)
        span_ref[:, DV * h : DV * (h + 1)] = value[0:SPAN]
        dec_ref[:, DV * h : DV * (h + 1)] = value[SPAN:COUNT]

    for c in exchange:
        c.wait_send()
    sent(*cring, *hring)
    for hs in range(1, SIDE):
        sent(back(hs))


def body(query, dec_query, cache_kv, span_kv, dec_kv, cache_fill, owner, slot, dec_len, w_uk, w_uv):
    fours = query.shape[0]
    q = jnp.concatenate(
        [query, dec_query, jnp.zeros((8 - fours - 1, query.shape[1]), query.dtype)], axis=0
    )
    kv = jnp.concatenate([span_kv, dec_kv], axis=0)
    kv = jnp.pad(kv, ((0, 8 - kv.shape[0]), (0, WIDE - kv.shape[1])))
    vmem = pl.BlockSpec(memory_space=pltpu.VMEM)
    smem = pl.BlockSpec(memory_space=pltpu.SMEM)
    dma = pltpu.SemaphoreType.DMA
    return pl.pallas_call(
        kernel,
        out_shape=(
            jax.ShapeDtypeStruct((SPAN, HEADS * DV), BF16),
            jax.ShapeDtypeStruct((ROWS, HEADS * DV), BF16),
            jax.ShapeDtypeStruct((POS, DC + DR), BF16),
        ),
        in_specs=[vmem, vmem, vmem, smem, vmem, vmem, smem, vmem, vmem],
        out_specs=(vmem, vmem, vmem),
        scratch_shapes=[
            pltpu.VMEM((SEQ, 8, SLICE), BF16),
            pltpu.VMEM((SEQ, 8, WIDE), BF16),
            pltpu.VMEM((SIDE, QROWS, WIDE), BF16),
            pltpu.VMEM((SIDE, QROWS // 2, 128), BF16),
            pltpu.VMEM((SIDE, POS, WIDE), BF16),
            pltpu.VMEM((SIDE, POS // 2, 128), BF16),
            pltpu.VMEM((128, WIDE), BF16),
            pltpu.VMEM((SIDE, QROWS, DC), F32),
            pltpu.VMEM((SIDE, QROWS, 1), F32),
            pltpu.VMEM((SIDE, QROWS, 1), F32),
            pltpu.VMEM((TILE, POS), F32),
            pltpu.VMEM((SIDE - 1, QROWS, DC), BF16),
            pltpu.VMEM((SIDE - 1, 8, 128), F32),
            pltpu.VMEM((SIDE - 1, QROWS, DC), BF16),
            pltpu.VMEM((SIDE - 1, 8, 128), F32),
            dma((2,)),
            dma((2 * (SEQ - 1),)),
            dma((2 * (SEQ - 1),)),
            dma((12,)),
            dma((12,)),
            dma((12,)),
            dma((12,)),
            dma((6,)),
            dma((6,)),
        ],
        compiler_params=pltpu.CompilerParams(
            collective_id=0, has_side_effects=True, vmem_limit_bytes=56 * 2**20
        ),
        cost_estimate=pl.CostEstimate(
            flops=2 * SIDE * SIDE * QROWS * POS * (DC + DR + DC),
            bytes_accessed=8 * 2**20,
            transcendentals=SIDE * SIDE * QROWS * POS,
        ),
    )(
        q, kv, cache_kv, cache_fill, owner.reshape(1, SPAN), slot.reshape(1, SPAN), dec_len, w_uk, w_uv,
    )


def solution(mesh):
    in_specs = (
        P(("grp", "seq"), None),
        P(("grp", "seq"), None),
        P(("grp", "seq"), None),
        P(("grp", "seq"), None),
        P(("grp", "seq"), None),
        P("grp"),
        P("grp"),
        P("grp"),
        P("grp"),
        P("seq", None, None),
        P("seq", None, None),
    )
    out_specs = (P("grp", "seq"), P("grp", "seq"), P(("grp", "seq"), None))
    return jax.shard_map(body, mesh=mesh, in_specs=in_specs, out_specs=out_specs, check_vma=False)
```

time: 599 us -> 102 us (0.17)
  blocking collectives: 341 us -> 0 us
  Pallas kernels: 0 us -> 92.1 us
  waiting for transfers between devices: 85.4 us -> 0 us
  matrix products: 48.4 us -> 0 us
  local copies, waits for them, and re-layouts: 41.7 us -> 6.18 us
  other arithmetic: 36.8 us -> 3.26 us
  starting transfers between devices: 27.6 us -> 0 us
  between operations: 14.4 us -> 0.66 us
    all_gather x2 -> x0, blocking collectives: 341 us -> none  [the longest x1 319 us: body(): lax.all_gather(dec_kv, 'seq', axis=0, tiled=True)]
    pallas_call x0 -> x1, Pallas kernels: none -> 92.1 us  [body(): pl.pallas_call(kernel, out_shape=(jax.ShapeDtypeStruct((SPAN, HEADS * DV)...]
    all_gather x1 -> x0, waiting for transfers between devices: 64.5 us -> none  [body(): everyone = lax.all_gather(absorbed, 'seq', axis=1, tiled=True)]
    dot_general x12 -> x0, matrix products: 48.4 us -> none  [the longest x4 26 us: block_partial(): jnp.einsum('qhc,pc->qhp', absorbed, keys, preferred_element_type=jnp.floa...]
    reduce_sum x8 -> x0, other arithmetic: 31.7 us -> none  [the longest x1 19 us: body(): acc = jnp.sum(factor[..., None] * outputs, axis=0)]
    all_to_all x5 -> x0, starting transfers between devices: 27.6 us -> none  [the longest x1 7.96 us: body(): lax.all_to_all(dec_query.reshape(dec_query.shape[0], heads_all, width), '...]
    another operation x1 -> x0, local copies, waits for them, and re-layouts: 21.3 us -> none  [body(): output[None]]
    all_to_all x5 -> x0, waiting for transfers between devices: 20.9 us -> none  [the longest x1 8.46 us: body(): lax.all_to_all(query.reshape(query.shape[0], heads_all, width), 'seq', sp...]
  transfers between devices with their start and end apart: 6 -> 0, of which waited for: 4 -> 0; matrix products, arithmetic and copies ran while one was open for 5% -> 0% of each run, Pallas kernels for 0% -> 0%
where the time goes in v1:
time: 102 us
  Pallas kernels  92.1 us (90%)
  local copies, waits for them, and re-layouts  6.18 us (6%)
  other arithmetic  3.26 us (3%)
    pallas_call x1, Pallas kernels, body(): pl.pallas_call(kernel, out_shape=(jax.ShapeDtypeStruct((SPAN, HEADS * DV)...  92.1 us
    unnamed x7, local copies, waits for them, and re-layouts  3.69 us
    pallas_call x1, local copies, waits for them, and re-layouts, body(): pl.pallas_call(kernel, out_shape=(jax.ShapeDtypeStruct((SPAN, HEADS * DV)...  2.41 us

profile of v1, /device:TPU:0, one launch (start us, length us, event | category | flops | bytes accessed | tf_op | source)
XLA Modules:
  0.0 102.2 jit_solution(17210276321405850643)
XLA Ops:
  0.6 0.1 pad.9.clone
  0.7 1.3 %fusion.5.kv_ref = bf16[8,640]{1,0:T(8,128)(2,1)} fusion(bf16[1,576]{1,0:T(2,128)(2,1)} %param.15, bf16[4,576]{1,0:T(4,128)(2,1)} %param.14), kind=kLoop, calls=%fused_computation.8 | loop fusion | flops 56320 | bytes 16000 | tf_op jit(solution)/shard_map/concatenate | solution.py:384
  2.0 1.9 %maximum_maximum_fusion.q_ref = bf16[8,24576]{1,0:T(8,128)(2,1)} fusion(bf16[1,24576]{1,0:T(2,128)(2,1)} %param.12, bf16[4,24576]{1,0:T(4,128)(2,1)} %param.11, bf16[8]{0:T(256)(128)(2,1)S(1)} %pad.9.clone), kind=kLoop, calls=%fused_computation | loop fusion | flops 1179648 | bytes 638992 | tf_op jit(solution)/shard_map/concatenate | solution.py:381
  4.0 2.4 %copy.14.cache_ref = bf16[1024,576]{1,0:T(8,128)(2,1)} copy(bf16[1024,576]{0,1:T(8,128)(2,1)} %param.13) | data formatting | bytes 2359296 | tf_op args[2]
  6.4 92.1 %shard_map.130 = (bf16[64,1024]{1,0:T(8,128)(2,1)}, bf16[16,1024]{1,0:T(8,128)(2,1)}, bf16[1024,576]{1,0:T(8,128)(2,1)}) custom-call(bf16[8,24576]{1,0:T(8,128)(2,1)} %maximum_maximum_fusion.q_ref, bf16[8,640]{1,0:T(8,128)(2,1)} %fusion.5.kv_ref, bf16[1024,576]{1,0:T(8,128)(2,1)} %copy.14.cache_ref, s32[16]{0:T(128)} %fill_ref.1, s32[1,64]{1,0:T(1,128)} %bitcast.2, ...), custom_call_target="tpu_custom_call" | custom-call | flops 22817013760 | bytes 8388608 | tf_op jit(solution)/shard_map/pallas_call | solution.py:389
  98.5 0.0 copy-start
  98.5 0.0 copy-start.1
  98.5 2.4 %copy.15 = bf16[1024,576]{0,1:T(8,128)(2,1)} copy(bf16[1024,576]{1,0:T(8,128)(2,1)} %get-tuple-element.5) | data formatting | bytes 2359296 | tf_op jit(solution)/shard_map/pallas_call | solution.py:389
  101.0 0.0 copy-done
  101.0 0.7 copy.18
  101.6 0.0 copy-done.1
  101.6 0.6 copy.19
  (1 shorter events, 0.0 us)
Async XLA Ops:
  98.5 2.4 %copy-start = (bf16[64,1024]{1,0:T(8,128)(2,1)S(1)}, bf16[64,1024]{1,0:T(8,128)(2,1)}, u32[]{:S(2)}) copy-start(bf16[64,1024]{1,0:T(8,128)(2,1)} %get-tuple-element.9) | copy-start | bytes 393220
  98.5 3.1 %copy-start.1 = (bf16[16,1024]{1,0:T(8,128)(2,1)S(1)}, bf16[16,1024]{1,0:T(8,128)(2,1)}, u32[]{:S(2)}) copy-start(bf16[16,1024]{1,0:T(8,128)(2,1)} %get-tuple-element.10) | copy-start | bytes 98308

commit v2 on v1

v2 whole, which is shorter than its diff:
```python
import functools
import math

import jax
import jax.numpy as jnp
from jax import lax
from jax.experimental import pallas as pl
from jax.experimental.pallas import tpu as pltpu
from jax.sharding import PartitionSpec as P

MESH = pl.DeviceIdType.MESH
F32 = jnp.float32
BF16 = jnp.bfloat16

SIDE = 4
SEQ = SIDE * SIDE
HEADS = 8
DN = 128
DR = 64
DC = 512
DV = 128
KEY = DC + DR
WIDE = DC + 128
POS = 1024
SPAN = 64
ROWS = 16
COUNT = SPAN + ROWS
BAND = HEADS // 2 * COUNT
SLICE = HEADS * (DN + DR)
MESSAGE = SLICE + WIDE
CHUNK = 256

SCALE2 = 0.1353 * math.log2(math.e)
LOW = -1e30

ORDER_BAND = (0, 1, 2, 7, 3, 6, 4, 5) + (4, 5, 2, 3, 6, 7) * 3 + (0, 1, 0, 1, 0, 1)
ORDER_KEYS = (0,) * 8 + (1,) * 6 + (3,) * 6 + (2,) * 6 + (1, 1, 3, 3, 2, 2)
STEPS = len(ORDER_BAND)
FINISH = 20


def dot(a, b):
    return jnp.dot(a, b, preferred_element_type=F32)


def dot_t(a, b):
    return lax.dot_general(a, b, (((1,), (1,)), ((), ())), preferred_element_type=F32)


def lane_mask(shape):
    return lax.broadcasted_iota(jnp.int32, shape, len(shape) - 1) < DR


def doubled():
    row = lax.broadcasted_iota(jnp.int32, (128, 128), 0)
    col = lax.broadcasted_iota(jnp.int32, (128, 128), 1)
    return jnp.where(row == lax.rem(col, DR), 1.0, 0.0).astype(BF16)


def pick(table, i):
    value = 0
    for at, entry in enumerate(table):
        if entry:
            value = value + entry * jnp.where(i == at, 1, 0)
    return value


def kernel(
    query_ref, dec_query_ref, span_kv_ref, dec_kv_ref, cache_ref, fill_ref, owner_ref, slot_ref, dlen_ref,
    uk_hbm, uv_hbm,
    out_ref, newc_hbm,
    rows8, kv8, a_out, a_in, q_all, qr_all, k_all, k_own, uk, uv, newc,
    acc, peak, total, score_a, score_b, best_a, best_b, weights, o_send, e_send, o_recv, e_recv,
    local_sem, a_send, a_recv, c_send, c_recv, h_send, h_recv, p_send, p_recv,
):
    seq, grp = lax.axis_index("seq"), lax.axis_index("grp")
    core = lax.rem(grp, 2)
    z, x = seq // SIDE, lax.rem(seq, SIDE)

    def along_z(d):
        return lax.rem(z + d + SIDE, SIDE) * SIDE + x

    def along_x(d):
        return z * SIDE + lax.rem(x + d + SIDE, SIDE)

    def cache_peer(d):
        return (1 - core) * along_z(d) + core * along_x(d)

    def head_peer(d):
        return core * along_z(d) + (1 - core) * along_x(d)

    def remote(src, dst, send, recv, peer):
        return pltpu.make_async_remote_copy(
            src_ref=src, dst_ref=dst, send_sem=send, recv_sem=recv,
            device_id=(peer, grp), device_id_type=MESH,
        )

    barrier = pltpu.get_barrier_semaphore()
    for d in range(1, SEQ):
        pl.semaphore_signal(
            barrier, inc=1, device_id=(lax.rem(seq + d, SEQ), grp), device_id_type=MESH
        )

    own_keys = pltpu.make_async_copy(cache_ref, k_all.at[0, pl.ds(0, KEY)], local_sem.at[0])
    own_uk = pltpu.make_async_copy(uk_hbm, uk, local_sem.at[1])
    own_uv = pltpu.make_async_copy(uv_hbm, uv, local_sem.at[2])
    own_keys.start()
    own_uk.start()
    own_uv.start()

    rows8[...] = jnp.zeros(rows8.shape, F32)
    rows8[0:4, :] = query_ref[...].astype(F32)
    rows8[4:5, :] = dec_query_ref[...].astype(F32)
    kv8[...] = jnp.zeros(kv8.shape, F32)
    kv8[0:4, 0:KEY] = span_kv_ref[...].astype(F32)
    kv8[4:5, 0:KEY] = dec_kv_ref[...].astype(F32)
    kv = kv8[...].astype(BF16)
    for s in range(SEQ):
        a_out[s, :, 0:SLICE] = rows8[:, s * SLICE : (s + 1) * SLICE].astype(BF16)
        a_out[s, :, SLICE:MESSAGE] = kv
    a_in[seq] = a_out[seq]

    pl.semaphore_wait(barrier, SEQ - 1)

    exchange = []
    for d in range(1, SEQ):
        peer = lax.rem(seq + d, SEQ)
        exchange.append(remote(a_out.at[peer], a_in.at[seq], a_send.at[d - 1], a_recv.at[d - 1], peer))
    for c in exchange:
        c.start()

    def ring(halves, send, recv, peer_of):
        count = len(halves(0, 0))

        def pair(i, src_slot, dst_slot, h, peer):
            src, dst = halves(src_slot, h), halves(dst_slot, h)
            return [
                remote(src[k], dst[k], send.at[count * i + k], recv.at[count * i + k], peer)
                for k in range(count)
            ]

        up, down = peer_of(1), peer_of(-1)
        first_up = pair(0, 0, 1, 0, up)
        first_down = pair(1, 0, 3, 1, down)
        second_up = pair(2, 0, 1, 1, up)
        second_down = pair(3, 0, 3, 0, down)
        onward_up = pair(4, 1, 2, 0, up)
        onward_down = pair(5, 3, 2, 1, down)
        return first_up, first_down, second_up, second_down, onward_up, onward_down

    def key_half(slot, h):
        return [k_all.at[slot, pl.ds(0, KEY), pl.ds(h * (POS // 2), POS // 2)]]

    def query_half(slot, h):
        return [q_all.at[2 * slot + h, pl.ds(0, BAND), pl.ds(0, DC)], qr_all.at[2 * slot + h]]

    def start(*groups):
        for g in groups:
            for c in g:
                c.start()

    def arrived(*groups):
        for g in groups:
            for c in g:
                c.wait_recv()

    def sent(*groups):
        for g in groups:
            for c in g:
                c.wait_send()

    cring = ring(key_half, c_send, c_recv, cache_peer)
    hring = ring(query_half, h_send, h_recv, head_peer)

    def unpack_keys(slot):
        k_all[slot, KEY:WIDE, :] = k_all[slot, DC:KEY, :]

    def unpack_queries(band):
        for p in range(HEADS // 4):
            both = qr_all[band, COUNT * p : COUNT * (p + 1), :].astype(F32)
            mask = lane_mask(both.shape)
            at = 2 * COUNT * p
            q_all[band, at : at + COUNT, DC:WIDE] = jnp.where(mask, both, 0.0).astype(BF16)
            q_all[band, at + COUNT : at + 2 * COUNT, DC:WIDE] = jnp.where(mask, 0.0, both).astype(BF16)

    own_keys.wait()
    start(cring[0], cring[1])
    unpack_keys(0)
    peak[...] = jnp.full(peak.shape, LOW, F32)
    total[...] = jnp.zeros(total.shape, F32)
    acc[...] = jnp.zeros(acc.shape, F32)
    e_send[...] = jnp.zeros(e_send.shape, F32)

    prow = lax.broadcasted_iota(jnp.int32, (COUNT, 128), 0)
    pcol = lax.broadcasted_iota(jnp.int32, (COUNT, 128), 1)
    place = jnp.where(prow < SPAN, 8 * (prow // 4) + lax.rem(prow, 4), 8 * (prow - SPAN) + 4)
    order = jnp.where(pcol == place, 1.0, 0.0).astype(BF16)
    own_uk.wait()
    for c in exchange:
        c.wait_recv()
    got = a_in[...].astype(F32).reshape(8 * SEQ, MESSAGE).astype(BF16)
    got = dot(order, got)
    for p in range(HEADS // 2):
        at = 3 * 128 * p
        t0, t1, t2 = (got[:, at + 128 * i : at + 128 * (i + 1)] for i in range(3))
        mask = lane_mask(t0.shape)
        nope = t0.astype(BF16)
        swapped = jnp.where(mask, t2, t1).astype(BF16)
        band, pair = p // 2, p % 2
        qr_all[band, COUNT * pair : COUNT * (pair + 1), :] = jnp.where(mask, t1, t2).astype(BF16)
        weight = uk[2 * p + 1]
        weight = jnp.concatenate([weight[DR:], weight[:DR]], axis=0)
        row0 = 2 * COUNT * pair
        q_all[band, row0 : row0 + COUNT, 0:DC] = dot(nope, uk[2 * p]).astype(BF16)
        q_all[band, row0 + COUNT : row0 + 2 * COUNT, 0:DC] = dot(swapped, weight).astype(BF16)
        if p == 1:
            start(hring[0])
        if p == 3:
            start(hring[1], hring[2], hring[3])
    unpack_queries(0)
    unpack_queries(1)

    kv_rows = got[:, SLICE:MESSAGE].astype(BF16)
    k_own[...] = jnp.zeros(k_own.shape, BF16)
    k_own[0:COUNT, 0:DC] = kv_rows[:, 0:DC]
    k_own[0:COUNT, DC:WIDE] = dot(kv_rows[:, DC:WIDE], doubled()).astype(BF16)

    def scores(band, ks, out, best):
        fill = fill_ref[cache_peer(-ks)]
        top = None
        for j in range(POS // CHUNK):
            at = slice(j * CHUNK, (j + 1) * CHUNK)
            s = dot(q_all[band], k_all[ks, :, at])
            local = lax.broadcasted_iota(jnp.int32, (1, CHUNK), 1) + j * CHUNK
            s = jnp.where(local < fill, s, LOW)
            out[:, at] = s
            for u in range(0, CHUNK, 128):
                top = s[:, u : u + 128] if top is None else jnp.maximum(top, s[:, u : u + 128])
            yield
        best[...] = top

    def attend(band, ks, now, later, ahead):
        score, best = now
        old = peak[band]
        top = jnp.maximum(old, jnp.max(best[...], axis=1, keepdims=True))
        keep = jnp.exp2((old - top) * SCALE2)
        add = None
        nxt = scores(*ahead, *later)
        for j in range(POS // CHUNK):
            next(nxt)
            at = slice(j * CHUNK, (j + 1) * CHUNK)
            e = jnp.exp2((score[:, at] - top) * SCALE2)
            weights[:, at] = e.astype(BF16)
            for u in range(0, CHUNK, 128):
                add = e[:, u : u + 128] if add is None else add + e[:, u : u + 128]
        next(nxt, None)
        out = dot_t(weights[...], k_all[ks, 0:DC, :])
        peak[band] = top
        total[band] = total[band] * keep + jnp.sum(add, axis=1, keepdims=True)
        acc[band] = acc[band] * keep + out

    eye = lax.broadcasted_iota(jnp.int32, (64, 128), 0) == lax.broadcasted_iota(jnp.int32, (64, 128), 1)

    def finish(band):
        t = total[band]
        o_send[band - 2] = (acc[band] * (1.0 / t)).astype(BF16)
        level = peak[band] * SCALE2 + jnp.log2(t)
        for i in range(BAND // 64):
            square = jnp.broadcast_to(level[64 * i : 64 * (i + 1)], (64, 128))
            e_send[band - 2, i : i + 1, :] = jnp.sum(jnp.where(eye, square, 0.0), axis=0, keepdims=True)

    def back(band):
        peer, i = head_peer(-(band // 2)), band - 2
        return [
            remote(o_send.at[i], o_recv.at[i], p_send.at[2 * i], p_recv.at[2 * i], peer),
            remote(e_send.at[i], e_recv.at[i], p_send.at[2 * i + 1], p_recv.at[2 * i + 1], peer),
        ]

    qrow = lax.broadcasted_iota(jnp.int32, (COUNT, 128), 0)
    kcol = lax.broadcasted_iota(jnp.int32, (COUNT, 128), 1)
    limit = jnp.where(qrow < SPAN, qrow + 1, 0)
    for r in range(ROWS):
        limit = jnp.where(qrow == SPAN + r, dlen_ref[r], limit)
    seen = (kcol < limit) | ((qrow >= SPAN) & (kcol == qrow))
    hidden = jnp.where(seen, 0.0, 1.0)
    hidden = jnp.concatenate([hidden] * (HEADS // 2), axis=0)
    for band in range(2):
        s = jnp.where(hidden > 0.5, LOW, dot_t(q_all[band], k_own[...]))
        top = jnp.max(s, axis=1, keepdims=True)
        e = jnp.exp2((s - top) * SCALE2)
        peak[band] = top
        total[band] = jnp.sum(e, axis=1, keepdims=True)
        acc[band] = dot(e.astype(BF16), k_own[:, 0:DC])

    target = jnp.where(owner_ref[...] == seq, slot_ref[...], -1)
    span_rows = kv_rows[0:SPAN, 0:KEY]

    @pl.loop(0, POS // 256)
    def _(i):
        at = pl.ds(pl.multiple_of(i * 256, 256), 256)
        local = lax.broadcasted_iota(jnp.int32, (256, SPAN), 0) + i * 256
        hot = jnp.where(local == target, 1.0, 0.0).astype(BF16)
        put = lax.dot_general(span_rows, hot, (((0,), (1,)), ((), ())), preferred_element_type=F32)
        any_hot = dot_t(jnp.ones((8, SPAN), BF16), hot)[0:1] > 0.5
        old = k_all[0, 0:KEY, at].astype(F32)
        newc[:, at] = jnp.where(any_hot, put, old).astype(BF16)

    put_cache = pltpu.make_async_copy(newc, newc_hbm, local_sem.at[3])
    put_cache.start()

    def before(i):
        @pl.when(i == 1)
        def _():
            arrived(hring[0], hring[1])
            start(hring[4], hring[5])
            start(cring[2], cring[3])
            unpack_queries(2)
            unpack_queries(7)

        @pl.when(i == 3)
        def _():
            arrived(hring[2], hring[3])
            unpack_queries(3)
            unpack_queries(6)
            arrived(cring[0], cring[1])
            start(cring[4], cring[5])

        @pl.when(i == 5)
        def _():
            arrived(hring[4], hring[5])
            unpack_queries(4)
            unpack_queries(5)

        @pl.when(i == 7)
        def _():
            arrived(cring[2])
            unpack_keys(1)

        @pl.when(i == 13)
        def _():
            arrived(cring[3])
            unpack_keys(3)

        @pl.when(i == 19)
        def _():
            arrived(cring[4], cring[5])
            unpack_keys(2)

    def after(i, band):
        @pl.when((i >= FINISH) & (i < FINISH + 6))
        def _():
            finish(band)
            start(back(band))

    a, b = (score_a, best_a), (score_b, best_b)
    for _ in scores(0, 0, *a):
        pass

    def step(i, now, later):
        before(i)
        band, ks = pick(ORDER_BAND, i), pick(ORDER_KEYS, i)
        ahead = jnp.minimum(i + 1, STEPS - 1)
        attend(band, ks, now, later, (pick(ORDER_BAND, ahead), pick(ORDER_KEYS, ahead)))
        after(i, band)

    @pl.loop(0, STEPS // 2)
    def _(i):
        step(2 * i, a, b)
        step(2 * i + 1, b, a)

    own_uv.wait()
    for half in range(2):
        levels = []
        for s in range(1, SIDE):
            i = 2 * s + half - 2
            arrived(back(i + 2))
            column = []
            for j in range(BAND // 64):
                square = jnp.broadcast_to(e_recv[i, j : j + 1, :], (64, 128))
                column.append(jnp.sum(jnp.where(eye, square, 0.0), axis=1, keepdims=True))
            levels.append(jnp.concatenate(column, axis=0))
        own_level = peak[half] * SCALE2 + jnp.log2(total[half])
        top = own_level
        for level in levels:
            top = jnp.maximum(top, level)
        weight = jnp.exp2(own_level - top)
        shares = [jnp.exp2(level - top) for level in levels]
        norm = 1.0 / (weight + shares[0] + shares[1] + shares[2])
        first = weight * norm / total[half]
        shares = [share * norm for share in shares]
        for h in range(HEADS // 2):
            rows = slice(COUNT * h, COUNT * (h + 1))
            latent = acc[half, rows, :] * first[rows]
            for s in range(SIDE - 1):
                latent = latent + o_recv[2 * s + half, rows, :].astype(F32) * shares[s][rows]
            head = HEADS // 2 * half + h
            value = dot(latent.astype(BF16), uv[head])
            out_ref[:, DV * head : DV * (head + 1)] = value.astype(BF16)

    put_cache.wait()
    for c in exchange:
        c.wait_send()
    sent(*cring, *hring)
    for band in range(2, 2 * SIDE):
        sent(back(band))


def hand_over(out_ref, cache_ref, span_ref, dec_ref, new_ref, out, cache, sem):
    half = KEY // 2
    ins = [pltpu.make_async_copy(out_ref, out, sem.at[0])]
    outs = [
        [
            pltpu.make_async_copy(out.at[pl.ds(0, SPAN)], span_ref, sem.at[3]),
            pltpu.make_async_copy(out.at[pl.ds(SPAN, ROWS)], dec_ref, sem.at[4]),
        ]
    ]
    for i in range(2):
        rows = pl.ds(i * half, half)
        ins.append(pltpu.make_async_copy(cache_ref.at[rows], cache.at[rows], sem.at[1 + i]))
        outs.append([pltpu.make_async_copy(cache.at[rows], new_ref.at[rows], sem.at[5 + i])])
    for c in ins:
        c.start()
    for c, then in zip(ins, outs):
        c.wait()
        for d in then:
            d.start()
    for then in outs:
        for d in then:
            d.wait()


def body(query, dec_query, cache_kv, span_kv, dec_kv, cache_fill, owner, slot, dec_len, w_uk, w_uv):
    vmem = pl.BlockSpec(memory_space=pltpu.VMEM)
    smem = pl.BlockSpec(memory_space=pltpu.SMEM)
    hbm = pl.BlockSpec(memory_space=pl.ANY)
    dma = pltpu.SemaphoreType.DMA
    shape = jax.ShapeDtypeStruct
    out, new_cache = pl.pallas_call(
        kernel,
        out_shape=(shape((COUNT, HEADS * DV), BF16), shape((KEY, POS), BF16)),
        in_specs=[vmem, vmem, vmem, vmem, hbm, smem, vmem, vmem, smem, hbm, hbm],
        out_specs=(vmem, hbm),
        scratch_shapes=[
            pltpu.VMEM((8, SEQ * SLICE), F32),
            pltpu.VMEM((8, WIDE), F32),
            pltpu.VMEM((SEQ, 8, MESSAGE), BF16),
            pltpu.VMEM((SEQ, 8, MESSAGE), BF16),
            pltpu.VMEM((2 * SIDE, BAND, WIDE), BF16),
            pltpu.VMEM((2 * SIDE, BAND // 2, 128), BF16),
            pltpu.VMEM((SIDE, WIDE, POS), BF16),
            pltpu.VMEM((128, WIDE), BF16),
            pltpu.VMEM((HEADS, DN, DC), BF16),
            pltpu.VMEM((HEADS, DC, DV), BF16),
            pltpu.VMEM((KEY, POS), BF16),
            pltpu.VMEM((2 * SIDE, BAND, DC), F32),
            pltpu.VMEM((2 * SIDE, BAND, 1), F32),
            pltpu.VMEM((2 * SIDE, BAND, 1), F32),
            pltpu.VMEM((BAND, POS), F32),
            pltpu.VMEM((BAND, POS), F32),
            pltpu.VMEM((BAND, 128), F32),
            pltpu.VMEM((BAND, 128), F32),
            pltpu.VMEM((BAND, POS), BF16),
            pltpu.VMEM((6, BAND, DC), BF16),
            pltpu.VMEM((6, 8, 128), F32),
            pltpu.VMEM((6, BAND, DC), BF16),
            pltpu.VMEM((6, 8, 128), F32),
            dma((4,)),
            dma((SEQ - 1,)),
            dma((SEQ - 1,)),
            dma((6,)),
            dma((6,)),
            dma((12,)),
            dma((12,)),
            dma((12,)),
            dma((12,)),
        ],
        compiler_params=pltpu.CompilerParams(
            collective_id=0, has_side_effects=True, vmem_limit_bytes=56 * 2**20
        ),
        cost_estimate=pl.CostEstimate(
            flops=2 * STEPS * BAND * POS * (KEY + DC),
            bytes_accessed=8 * 2**20,
            transcendentals=STEPS * BAND * POS,
        ),
    )(
        query, dec_query, span_kv, dec_kv, cache_kv.T, cache_fill,
        owner.reshape(1, SPAN), slot.reshape(1, SPAN), dec_len, w_uk, w_uv,
    )
    span_out, dec_out, new_cache = pl.pallas_call(
        hand_over,
        out_shape=(
            shape((SPAN, HEADS * DV), BF16),
            shape((ROWS, HEADS * DV), BF16),
            shape((KEY, POS), BF16),
        ),
        in_specs=[hbm, hbm],
        out_specs=(hbm, hbm, hbm),
        scratch_shapes=[
            pltpu.VMEM((COUNT, HEADS * DV), BF16),
            pltpu.VMEM((KEY, POS), BF16),
            dma((7,)),
        ],
        compiler_params=pltpu.CompilerParams(vmem_limit_bytes=60 * 2**20),
        cost_estimate=pl.CostEstimate(flops=0, bytes_accessed=3 * 2**20, transcendentals=0),
    )(out, new_cache)
    return span_out, dec_out, new_cache.T


def solution(mesh):
    in_specs = (
        P(("grp", "seq"), None),
        P(("grp", "seq"), None),
        P(("grp", "seq"), None),
        P(("grp", "seq"), None),
        P(("grp", "seq"), None),
        P("grp"),
        P("grp"),
        P("grp"),
        P("grp"),
        P("seq", None, None),
        P("seq", None, None),
    )
    out_specs = (P("grp", "seq"), P("grp", "seq"), P(("grp", "seq"), None))
    return jax.shard_map(body, mesh=mesh, in_specs=in_specs, out_specs=out_specs, check_vma=False)
```

time: 102 us -> 83.3 us (0.82)
  Pallas kernels: 92.1 us -> 82.1 us
  local copies, waits for them, and re-layouts: 6.18 us -> 0 us
  other arithmetic: 3.26 us -> 0 us
    pallas_call x1 -> x2, Pallas kernels: 92.1 us -> 82.1 us  [the longest x1 79.9 us: body(): pl.pallas_call(kernel, out_shape=(shape((COUNT, HEADS * DV), BF16), shape...]
    unnamed x7 -> x0, local copies, waits for them, and re-layouts: 3.69 us -> none
    concatenate x2 -> x0, other arithmetic: 3.26 us -> none  [the longest x1 1.94 us: body(): jnp.concatenate([query, dec_query, jnp.zeros((8 - fours - 1, query.shape[...]
    pallas_call x1 -> x0, local copies, waits for them, and re-layouts: 2.41 us -> none  [body(): pl.pallas_call(kernel, out_shape=(jax.ShapeDtypeStruct((SPAN, HEADS * DV)...]
where the time goes in v2:
time: 83.3 us; the launch traced here: 82.8 us
  Pallas kernels  82.1 us (99%)
    pallas_call x1, Pallas kernels, body(): pl.pallas_call(kernel, out_shape=(shape((COUNT, HEADS * DV), BF16), shape...  79.9 us
    pallas_call x1, Pallas kernels, body(): pl.pallas_call(hand_over, out_shape=(shape((SPAN, HEADS * DV), BF16), sha...  2.22 us

profile of v2, /device:TPU:0, one launch (start us, length us, event | category | flops | bytes accessed | tf_op | source)
XLA Modules:
  0.0 82.8 jit_solution(16968045212876689047)
XLA Ops:
  0.6 79.9 %shard_map.130 = (bf16[80,1024]{1,0:T(8,128)(2,1)}, bf16[576,1024]{1,0:T(8,128)(2,1)}) custom-call(bf16[4,24576]{1,0:T(4,128)(2,1)} %query_ref.1, bf16[1,24576]{1,0:T(2,128)(2,1)} %dec_query_ref.1, bf16[4,576]{1,0:T(4,128)(2,1)} %span_kv_ref.1, bf16[1,576]{1,0:T(2,128)(2,1)} %dec_kv_ref.1, bf16[576,1024]{1,0:T(8,128)(2,1)} %bitcast.4, s32[16]{0:T(128)} %fill_ref.1, ...), custom_call_target="tpu_custom_call" | custom-call | flops 22817013760 | bytes 8388608 | tf_op jit(solution)/shard_map/pallas_call | solution.py:438
  80.6 2.2 %shard_map.131 = (bf16[64,1024]{1,0:T(8,128)(2,1)}, bf16[16,1024]{1,0:T(8,128)(2,1)}, bf16[576,1024]{1,0:T(8,128)(2,1)}) custom-call(bf16[80,1024]{1,0:T(8,128)(2,1)} %get-tuple-element.8.out_ref, bf16[576,1024]{1,0:T(8,128)(2,1)} %get-tuple-element.9.cache_ref), custom_call_target="tpu_custom_call" | custom-call | bytes 3145728 | tf_op jit(solution)/shard_map/pallas_call | solution.py:489

commit v3 on v2

--- a/solution.py
+++ b/solution.py
@@ -27,14 +27,15 @@
 COUNT = SPAN + ROWS
 BAND = HEADS // 2 * COUNT
 SLICE = HEADS * (DN + DR)
-MESSAGE = SLICE + WIDE
 CHUNK = 256
 
 SCALE2 = 0.1353 * math.log2(math.e)
 LOW = -1e30
 
+PIECES = ((0, 0), (0, 1), (1, 0), (3, 1), (1, 1), (3, 0), (2, 0), (2, 1))
+HALF = POS // 2
 ORDER_BAND = (0, 1, 2, 7, 3, 6, 4, 5) + (4, 5, 2, 3, 6, 7) * 3 + (0, 1, 0, 1, 0, 1)
-ORDER_KEYS = (0,) * 8 + (1,) * 6 + (3,) * 6 + (2,) * 6 + (1, 1, 3, 3, 2, 2)
+ORDER_KEYS = (0,) * 8 + (1,) * 6 + (2,) * 6 + (3,) * 6 + (1, 1, 2, 2, 3, 3)
 STEPS = len(ORDER_BAND)
 FINISH = 20
 
@@ -58,18 +59,18 @@
 
 
 def pick(table, i):
-    value = 0
-    for at, entry in enumerate(table):
-        if entry:
-            value = value + entry * jnp.where(i == at, 1, 0)
-    return value
+    word = None
+    for lo in reversed(range(0, len(table), 8)):
+        packed = sum(entry << (4 * at) for at, entry in enumerate(table[lo : lo + 8]))
+        word = jnp.int32(packed) if word is None else jnp.where(i < lo + 8, jnp.int32(packed), word)
+    return lax.shift_right_logical(word, 4 * lax.rem(i, 8)) & 7
 
 
 def kernel(
     query_ref, dec_query_ref, span_kv_ref, dec_kv_ref, cache_ref, fill_ref, owner_ref, slot_ref, dlen_ref,
     uk_hbm, uv_hbm,
     out_ref, newc_hbm,
-    rows8, kv8, a_out, a_in, q_all, qr_all, k_all, k_own, uk, uv, newc,
+    rows8, kv8, a_out, a_in, kv_out, kv_in, q_all, qr_all, k_all, k_own, uk, uv, newc,
     acc, peak, total, score_a, score_b, best_a, best_b, weights, o_send, e_send, o_recv, e_recv,
     local_sem, a_send, a_recv, c_send, c_recv, h_send, h_recv, p_send, p_recv,
 ):
@@ -101,10 +102,16 @@
             barrier, inc=1, device_id=(lax.rem(seq + d, SEQ), grp), device_id_type=MESH
         )
 
-    own_keys = pltpu.make_async_copy(cache_ref, k_all.at[0, pl.ds(0, KEY)], local_sem.at[0])
+    own_keys = [
+        pltpu.make_async_copy(
+            cache_ref.at[:, pl.ds(h * HALF, HALF)], k_all.at[h, pl.ds(0, KEY)], local_sem.at[4 * h]
+        )
+        for h in range(2)
+    ]
     own_uk = pltpu.make_async_copy(uk_hbm, uk, local_sem.at[1])
     own_uv = pltpu.make_async_copy(uv_hbm, uv, local_sem.at[2])
-    own_keys.start()
+    for c in own_keys:
+        c.start()
     own_uk.start()
     own_uv.start()
 
@@ -114,18 +121,21 @@
     kv8[...] = jnp.zeros(kv8.shape, F32)
     kv8[0:4, 0:KEY] = span_kv_ref[...].astype(F32)
     kv8[4:5, 0:KEY] = dec_kv_ref[...].astype(F32)
-    kv = kv8[...].astype(BF16)
+    kv_out[...] = kv8[...].astype(BF16)
     for s in range(SEQ):
-        a_out[s, :, 0:SLICE] = rows8[:, s * SLICE : (s + 1) * SLICE].astype(BF16)
-        a_out[s, :, SLICE:MESSAGE] = kv
+        a_out[s] = rows8[:, s * SLICE : (s + 1) * SLICE].astype(BF16)
     a_in[seq] = a_out[seq]
+    kv_in[seq] = kv_out[...]
 
     pl.semaphore_wait(barrier, SEQ - 1)
 
-    exchange = []
+    exchange, exchange_kv = [], []
     for d in range(1, SEQ):
         peer = lax.rem(seq + d, SEQ)
         exchange.append(remote(a_out.at[peer], a_in.at[seq], a_send.at[d - 1], a_recv.at[d - 1], peer))
+        exchange_kv.append(
+            remote(kv_out, kv_in.at[seq], a_send.at[SEQ + d - 2], a_recv.at[SEQ + d - 2], peer)
+        )
     for c in exchange:
         c.start()
 
@@ -149,7 +159,7 @@
         return first_up, first_down, second_up, second_down, onward_up, onward_down
 
     def key_half(slot, h):
-        return [k_all.at[slot, pl.ds(0, KEY), pl.ds(h * (POS // 2), POS // 2)]]
+        return [k_all.at[PIECES.index((slot, h)), pl.ds(0, KEY)]]
 
     def query_half(slot, h):
         return [q_all.at[2 * slot + h, pl.ds(0, BAND), pl.ds(0, DC)], qr_all.at[2 * slot + h]]
@@ -172,8 +182,9 @@
     cring = ring(key_half, c_send, c_recv, cache_peer)
     hring = ring(query_half, h_send, h_recv, head_peer)
 
-    def unpack_keys(slot):
-        k_all[slot, KEY:WIDE, :] = k_all[slot, DC:KEY, :]
+    def unpack_keys(block):
+        for piece in (2 * block, 2 * block + 1):
+            k_all[piece, KEY:WIDE, :] = k_all[piece, DC:KEY, :]
 
     def unpack_queries(band):
         for p in range(HEADS // 4):
@@ -183,7 +194,10 @@
             q_all[band, at : at + COUNT, DC:WIDE] = jnp.where(mask, both, 0.0).astype(BF16)
             q_all[band, at + COUNT : at + 2 * COUNT, DC:WIDE] = jnp.where(mask, 0.0, both).astype(BF16)
 
-    own_keys.wait()
+    for c in own_keys:
+        c.wait()
+    for c in exchange_kv:
+        c.start()
     start(cring[0], cring[1])
     unpack_keys(0)
     peak[...] = jnp.full(peak.shape, LOW, F32)
@@ -198,7 +212,7 @@
     own_uk.wait()
     for c in exchange:
         c.wait_recv()
-    got = a_in[...].astype(F32).reshape(8 * SEQ, MESSAGE).astype(BF16)
+    got = a_in[...].astype(F32).reshape(8 * SEQ, SLICE).astype(BF16)
     got = dot(order, got)
     for p in range(HEADS // 2):
         at = 3 * 128 * p
@@ -220,26 +234,31 @@
     unpack_queries(0)
     unpack_queries(1)
 
-    kv_rows = got[:, SLICE:MESSAGE].astype(BF16)
+    for c in exchange_kv:
+        c.wait_recv()
+    kv_rows = kv_in[...].astype(F32).reshape(8 * SEQ, WIDE).astype(BF16)
+    kv_rows = dot(order, kv_rows).astype(BF16)
     k_own[...] = jnp.zeros(k_own.shape, BF16)
     k_own[0:COUNT, 0:DC] = kv_rows[:, 0:DC]
     k_own[0:COUNT, DC:WIDE] = dot(kv_rows[:, DC:WIDE], doubled()).astype(BF16)
 
-    def scores(band, ks, out, best):
-        fill = fill_ref[cache_peer(-ks)]
+    def scores(band, block, out, best):
         top = None
-        for j in range(POS // CHUNK):
-            at = slice(j * CHUNK, (j + 1) * CHUNK)
-            s = dot(q_all[band], k_all[ks, :, at])
-            local = lax.broadcasted_iota(jnp.int32, (1, CHUNK), 1) + j * CHUNK
-            s = jnp.where(local < fill, s, LOW)
-            out[:, at] = s
-            for u in range(0, CHUNK, 128):
-                top = s[:, u : u + 128] if top is None else jnp.maximum(top, s[:, u : u + 128])
-            yield
+        for side in range(2):
+            slot = pick([PIECES[2 * b + side][0] for b in range(SIDE)], block)
+            half = pick([PIECES[2 * b + side][1] for b in range(SIDE)], block)
+            fill = fill_ref[cache_peer(-slot)] - half * HALF
+            for j in range(0, HALF, CHUNK):
+                s = dot(q_all[band], k_all[2 * block + side, :, j : j + CHUNK])
+                local = lax.broadcasted_iota(jnp.int32, (1, CHUNK), 1) + j
+                s = jnp.where(local < fill, s, LOW)
+                out[:, side * HALF + j : side * HALF + j + CHUNK] = s
+                for u in range(0, CHUNK, 128):
+                    top = s[:, u : u + 128] if top is None else jnp.maximum(top, s[:, u : u + 128])
+                yield
         best[...] = top
 
-    def attend(band, ks, now, later, ahead):
+    def attend(band, block, now, later, ahead):
         score, best = now
         old = peak[band]
         top = jnp.maximum(old, jnp.max(best[...], axis=1, keepdims=True))
@@ -254,7 +273,8 @@
             for u in range(0, CHUNK, 128):
                 add = e[:, u : u + 128] if add is None else add + e[:, u : u + 128]
         next(nxt, None)
-        out = dot_t(weights[...], k_all[ks, 0:DC, :])
+        out = dot_t(weights[:, 0:HALF], k_all[2 * block, 0:DC, :])
+        out += dot_t(weights[:, HALF:POS], k_all[2 * block + 1, 0:DC, :])
         peak[band] = top
         total[band] = total[band] * keep + jnp.sum(add, axis=1, keepdims=True)
         acc[band] = acc[band] * keep + out
@@ -297,13 +317,14 @@
 
     @pl.loop(0, POS // 256)
     def _(i):
-        at = pl.ds(pl.multiple_of(i * 256, 256), 256)
+        piece = i // 2
         local = lax.broadcasted_iota(jnp.int32, (256, SPAN), 0) + i * 256
         hot = jnp.where(local == target, 1.0, 0.0).astype(BF16)
         put = lax.dot_general(span_rows, hot, (((0,), (1,)), ((), ())), preferred_element_type=F32)
         any_hot = dot_t(jnp.ones((8, SPAN), BF16), hot)[0:1] > 0.5
-        old = k_all[0, 0:KEY, at].astype(F32)
-        newc[:, at] = jnp.where(any_hot, put, old).astype(BF16)
+        at = pl.ds(pl.multiple_of(lax.rem(i, 2) * 256, 256), 256)
+        old = k_all[piece, 0:KEY, at].astype(F32)
+        newc[:, pl.ds(pl.multiple_of(i * 256, 256), 256)] = jnp.where(any_hot, put, old).astype(BF16)
 
     put_cache = pltpu.make_async_copy(newc, newc_hbm, local_sem.at[3])
     put_cache.start()
@@ -313,17 +334,15 @@
         def _():
             arrived(hring[0], hring[1])
             start(hring[4], hring[5])
-            start(cring[2], cring[3])
             unpack_queries(2)
             unpack_queries(7)
 
         @pl.when(i == 3)
         def _():
             arrived(hring[2], hring[3])
+            start(cring[2], cring[3])
             unpack_queries(3)
             unpack_queries(6)
-            arrived(cring[0], cring[1])
-            start(cring[4], cring[5])
 
         @pl.when(i == 5)
         def _():
@@ -333,18 +352,19 @@
 
         @pl.when(i == 7)
         def _():
-            arrived(cring[2])
+            arrived(cring[0], cring[1])
+            start(cring[4], cring[5])
             unpack_keys(1)
 
         @pl.when(i == 13)
         def _():
-            arrived(cring[3])
+            arrived(cring[2], cring[3])
+            unpack_keys(2)
+
+        @pl.when(i == 19)
+        def _():
+            arrived(cring[4], cring[5])
             unpack_keys(3)
-
-        @pl.when(i == 19)
-        def _():
-            arrived(cring[4], cring[5])
-            unpack_keys(2)
 
     def after(i, band):
         @pl.when((i >= FINISH) & (i < FINISH + 6))
@@ -398,7 +418,7 @@
             out_ref[:, DV * head : DV * (head + 1)] = value.astype(BF16)
 
     put_cache.wait()
-    for c in exchange:
+    for c in exchange + exchange_kv:
         c.wait_send()
     sent(*cring, *hring)
     for band in range(2, 2 * SIDE):
@@ -443,11 +463,13 @@
         scratch_shapes=[
             pltpu.VMEM((8, SEQ * SLICE), F32),
             pltpu.VMEM((8, WIDE), F32),
-            pltpu.VMEM((SEQ, 8, MESSAGE), BF16),
-            pltpu.VMEM((SEQ, 8, MESSAGE), BF16),
+            pltpu.VMEM((SEQ, 8, SLICE), BF16),
+            pltpu.VMEM((SEQ, 8, SLICE), BF16),
+            pltpu.VMEM((8, WIDE), BF16),
+            pltpu.VMEM((SEQ, 8, WIDE), BF16),
             pltpu.VMEM((2 * SIDE, BAND, WIDE), BF16),
             pltpu.VMEM((2 * SIDE, BAND // 2, 128), BF16),
-            pltpu.VMEM((SIDE, WIDE, POS), BF16),
+            pltpu.VMEM((2 * SIDE, WIDE, HALF), BF16),
             pltpu.VMEM((128, WIDE), BF16),
             pltpu.VMEM((HEADS, DN, DC), BF16),
             pltpu.VMEM((HEADS, DC, DV), BF16),
@@ -464,9 +486,9 @@
             pltpu.VMEM((6, 8, 128), F32),
             pltpu.VMEM((6, BAND, DC), BF16),
             pltpu.VMEM((6, 8, 128), F32),
-            dma((4,)),
-            dma((SEQ - 1,)),
-            dma((SEQ - 1,)),
+            dma((5,)),
+            dma((2 * (SEQ - 1),)),
+            dma((2 * (SEQ - 1),)),
             dma((6,)),
             dma((6,)),
             dma((12,)),

time: 83.3 us -> 78.4 us (0.941)
  Pallas kernels: 82.1 us -> 77.5 us
    pallas_call x1, Pallas kernels: 79.9 us -> 75.3 us  [body(): pl.pallas_call(kernel, out_shape=(shape((COUNT, HEADS * DV), BF16), shape...]
where the time goes in v3:
time: 78.4 us; the launch traced here: 78.2 us
  Pallas kernels  77.5 us (99%)
    pallas_call x1, Pallas kernels, body(): pl.pallas_call(kernel, out_shape=(shape((COUNT, HEADS * DV), BF16), shape...  75.3 us
    pallas_call x1, Pallas kernels, body(): pl.pallas_call(hand_over, out_shape=(shape((SPAN, HEADS * DV), BF16), sha...  2.22 us

profile of v3, /device:TPU:0, one launch (start us, length us, event | category | flops | bytes accessed | tf_op | source)
XLA Modules:
  0.0 78.2 jit_solution(18235581104950681424)
XLA Ops:
  0.6 75.3 %shard_map.130 = (bf16[80,1024]{1,0:T(8,128)(2,1)}, bf16[576,1024]{1,0:T(8,128)(2,1)}) custom-call(bf16[4,24576]{1,0:T(4,128)(2,1)} %query_ref.1, bf16[1,24576]{1,0:T(2,128)(2,1)} %dec_query_ref.1, bf16[4,576]{1,0:T(4,128)(2,1)} %span_kv_ref.1, bf16[1,576]{1,0:T(2,128)(2,1)} %dec_kv_ref.1, bf16[576,1024]{1,0:T(8,128)(2,1)} %bitcast.4, s32[16]{0:T(128)} %fill_ref.1, ...), custom_call_target="tpu_custom_call" | custom-call | flops 22817013760 | bytes 8388608 | tf_op jit(solution)/shard_map/pallas_call | solution.py:458
  75.9 2.2 %shard_map.131 = (bf16[64,1024]{1,0:T(8,128)(2,1)}, bf16[16,1024]{1,0:T(8,128)(2,1)}, bf16[576,1024]{1,0:T(8,128)(2,1)}) custom-call(bf16[80,1024]{1,0:T(8,128)(2,1)} %get-tuple-element.8.out_ref, bf16[576,1024]{1,0:T(8,128)(2,1)} %get-tuple-element.9.cache_ref), custom_call_target="tpu_custom_call" | custom-call | bytes 3145728 | tf_op jit(solution)/shard_map/pallas_call | solution.py:511

commit v4 on v3

--- a/solution.py
+++ b/solution.py
@@ -34,10 +34,10 @@
 
 PIECES = ((0, 0), (0, 1), (1, 0), (3, 1), (1, 1), (3, 0), (2, 0), (2, 1))
 HALF = POS // 2
-ORDER_BAND = (0, 1, 2, 7, 3, 6, 4, 5) + (4, 5, 2, 3, 6, 7) * 3 + (0, 1, 0, 1, 0, 1)
-ORDER_KEYS = (0,) * 8 + (1,) * 6 + (2,) * 6 + (3,) * 6 + (1, 1, 2, 2, 3, 3)
+ORDER_BAND = (0, 1, 0, 1, 2, 7, 2, 7, 3, 6, 3, 6, 4, 5, 4, 5) + (4, 5, 3, 6, 2, 7) * 2 + (0, 1) * 2
+ORDER_KEYS = (0, 0, 1, 1) * 4 + (2,) * 6 + (3,) * 6 + (2, 2, 3, 3)
 STEPS = len(ORDER_BAND)
-FINISH = 20
+FINISH = 22
 
 
 def dot(a, b):
@@ -264,7 +264,7 @@
         top = jnp.maximum(old, jnp.max(best[...], axis=1, keepdims=True))
         keep = jnp.exp2((old - top) * SCALE2)
         add = None
-        nxt = scores(*ahead, *later)
+        nxt = scores(*ahead, *later) if ahead is not None else iter((None,) * 4)
         for j in range(POS // CHUNK):
             next(nxt)
             at = slice(j * CHUNK, (j + 1) * CHUNK)
@@ -281,20 +281,41 @@
 
     eye = lax.broadcasted_iota(jnp.int32, (64, 128), 0) == lax.broadcasted_iota(jnp.int32, (64, 128), 1)
 
-    def finish(band):
-        t = total[band]
-        o_send[band - 2] = (acc[band] * (1.0 / t)).astype(BF16)
-        level = peak[band] * SCALE2 + jnp.log2(t)
+    def rows_to_lanes(level, ref, index):
         for i in range(BAND // 64):
             square = jnp.broadcast_to(level[64 * i : 64 * (i + 1)], (64, 128))
-            e_send[band - 2, i : i + 1, :] = jnp.sum(jnp.where(eye, square, 0.0), axis=0, keepdims=True)
+            ref[index, i : i + 1, :] = jnp.sum(jnp.where(eye, square, 0.0), axis=0, keepdims=True)
+
+    def lanes_to_rows(ref, index):
+        column = []
+        for i in range(BAND // 64):
+            square = jnp.broadcast_to(ref[index, i : i + 1, :], (64, 128))
+            column.append(jnp.sum(jnp.where(eye, square, 0.0), axis=1, keepdims=True))
+        return jnp.concatenate(column, axis=0)
 
     def back(band):
-        peer, i = head_peer(-(band // 2)), band - 2
+        peer, i = head_peer(jnp.where(band <= 4, -1, 1)), band - 2
         return [
             remote(o_send.at[i], o_recv.at[i], p_send.at[2 * i], p_recv.at[2 * i], peer),
             remote(e_send.at[i], e_recv.at[i], p_send.at[2 * i + 1], p_recv.at[2 * i + 1], peer),
         ]
+
+    def finish(band):
+        t = total[band]
+        o_send[band - 2] = (acc[band] * (1.0 / t)).astype(BF16)
+        rows_to_lanes(peak[band] * SCALE2 + jnp.log2(t), e_send, band - 2)
+
+    def finish_both(band, other):
+        arrived(back(other))
+        t = total[band]
+        here, there = peak[band] * SCALE2 + jnp.log2(t), lanes_to_rows(e_recv, other - 2)
+        top = jnp.maximum(here, there)
+        w_here, w_there = jnp.exp2(here - top), jnp.exp2(there - top)
+        both = w_here + w_there
+        norm = 1.0 / both
+        part = acc[band] * (w_here * norm / t) + o_recv[other - 2].astype(F32) * (w_there * norm)
+        o_send[band - 2] = part.astype(BF16)
+        rows_to_lanes(top + jnp.log2(both), e_send, band - 2)
 
     qrow = lax.broadcasted_iota(jnp.int32, (COUNT, 128), 0)
     kcol = lax.broadcasted_iota(jnp.int32, (COUNT, 128), 1)
@@ -329,90 +350,107 @@
     put_cache = pltpu.make_async_copy(newc, newc_hbm, local_sem.at[3])
     put_cache.start()
 
-    def before(i):
-        @pl.when(i == 1)
+    def event(g):
+        @pl.when(g == 2)
+        def _():
+            arrived(cring[0], cring[1])
+            unpack_keys(1)
+
+        @pl.when(g == 4)
         def _():
             arrived(hring[0], hring[1])
             start(hring[4], hring[5])
             unpack_queries(2)
             unpack_queries(7)
 
-        @pl.when(i == 3)
+        @pl.when(g == 8)
         def _():
             arrived(hring[2], hring[3])
             start(cring[2], cring[3])
             unpack_queries(3)
             unpack_queries(6)
 
-        @pl.when(i == 5)
+        @pl.when(g == 12)
         def _():
             arrived(hring[4], hring[5])
+            start(cring[4], cring[5])
             unpack_queries(4)
             unpack_queries(5)
 
-        @pl.when(i == 7)
-        def _():
-            arrived(cring[0], cring[1])
-            start(cring[4], cring[5])
-            unpack_keys(1)
-
-        @pl.when(i == 13)
+        @pl.when(g == 16)
         def _():
             arrived(cring[2], cring[3])
             unpack_keys(2)
 
-        @pl.when(i == 19)
+        @pl.when(g == 22)
         def _():
             arrived(cring[4], cring[5])
             unpack_keys(3)
 
-    def after(i, band):
-        @pl.when((i >= FINISH) & (i < FINISH + 6))
-        def _():
-            finish(band)
+        def leave(i):
+            band = pick(ORDER_BAND, i)
+
+            @pl.when(i < FINISH + 4)
+            def _():
+                finish(band)
+
+            @pl.when(i >= FINISH + 4)
+            def _():
+                finish_both(band, jnp.where(band == 2, 4, 5))
+
             start(back(band))
+
+        for late in (3, 2):
+            i = g - late
+
+            @pl.when((i >= FINISH) & (i < FINISH + 6) & ((late == 2) | (i > FINISH)))
+            def _():
+                leave(i)
 
     a, b = (score_a, best_a), (score_b, best_b)
     for _ in scores(0, 0, *a):
         pass
 
-    def step(i, now, later):
-        before(i)
-        band, ks = pick(ORDER_BAND, i), pick(ORDER_KEYS, i)
-        ahead = jnp.minimum(i + 1, STEPS - 1)
-        attend(band, ks, now, later, (pick(ORDER_BAND, ahead), pick(ORDER_KEYS, ahead)))
-        after(i, band)
-
-    @pl.loop(0, STEPS // 2)
-    def _(i):
-        step(2 * i, a, b)
-        step(2 * i + 1, b, a)
+    def of(i):
+        return pick(ORDER_BAND, i), pick(ORDER_KEYS, i)
+
+    attend(0, 0, a, b, (ORDER_BAND[1], ORDER_KEYS[1]))
+
+    @pl.loop(0, STEPS // 2 - 1)
+    def _(j):
+        i = 2 * j + 1
+        g = i + 1
+
+        @pl.when((g <= 4) | (g == 8) | (g == 12) | (g == 16) | (g >= FINISH))
+        def _():
+            event(g)
+
+        attend(*of(i), b, a, of(i + 1))
+        attend(*of(i + 1), a, b, of(i + 2))
+
+    attend(ORDER_BAND[-1], ORDER_KEYS[-1], b, a, None)
 
     own_uv.wait()
     for half in range(2):
+        parts = (half, 4 + half)
         levels = []
-        for s in range(1, SIDE):
-            i = 2 * s + half - 2
+        for i in parts:
             arrived(back(i + 2))
-            column = []
-            for j in range(BAND // 64):
-                square = jnp.broadcast_to(e_recv[i, j : j + 1, :], (64, 128))
-                column.append(jnp.sum(jnp.where(eye, square, 0.0), axis=1, keepdims=True))
-            levels.append(jnp.concatenate(column, axis=0))
+            levels.append(lanes_to_rows(e_recv, i))
         own_level = peak[half] * SCALE2 + jnp.log2(total[half])
         top = own_level
         for level in levels:
             top = jnp.maximum(top, level)
         weight = jnp.exp2(own_level - top)
         shares = [jnp.exp2(level - top) for level in levels]
-        norm = 1.0 / (weight + shares[0] + shares[1] + shares[2])
+        norm = 1.0 / (weight + shares[0] + shares[1])
         first = weight * norm / total[half]
         shares = [share * norm for share in shares]
         for h in range(HEADS // 2):
             rows = slice(COUNT * h, COUNT * (h + 1))
             latent = acc[half, rows, :] * first[rows]
-            for s in range(SIDE - 1):
-                latent = latent + o_recv[2 * s + half, rows, :].astype(F32) * shares[s][rows]
+            for i, share in zip(parts, shares):
+                latent = latent + o_recv[i, rows, :].astype(F32) * share[rows]
             head = HEADS // 2 * half + h
             value = dot(latent.astype(BF16), uv[head])
             out_ref[:, DV * head : DV * (head + 1)] = value.astype(BF16)

time: 78.4 us -> 74.6 us (0.952)
  Pallas kernels: 77.5 us -> 73.8 us
    pallas_call x1, Pallas kernels: 75.3 us -> 71.6 us  [body(): pl.pallas_call(kernel, out_shape=(shape((COUNT, HEADS * DV), BF16), shape...]
where the time goes in v4:
time: 74.6 us; the launch traced here: 74.4 us
  Pallas kernels  73.8 us (99%)
    pallas_call x1, Pallas kernels, body(): pl.pallas_call(kernel, out_shape=(shape((COUNT, HEADS * DV), BF16), shape...  71.6 us
    pallas_call x1, Pallas kernels, body(): pl.pallas_call(hand_over, out_shape=(shape((SPAN, HEADS * DV), BF16), sha...  2.22 us

profile of v4, /device:TPU:0, one launch (start us, length us, event | category | flops | bytes accessed | tf_op | source)
XLA Modules:
  0.0 74.4 jit_solution(801152931776497215)
XLA Ops:
  0.6 71.6 %shard_map.130 = (bf16[80,1024]{1,0:T(8,128)(2,1)}, bf16[576,1024]{1,0:T(8,128)(2,1)}) custom-call(bf16[4,24576]{1,0:T(4,128)(2,1)} %query_ref.1, bf16[1,24576]{1,0:T(2,128)(2,1)} %dec_query_ref.1, bf16[4,576]{1,0:T(4,128)(2,1)} %span_kv_ref.1, bf16[1,576]{1,0:T(2,128)(2,1)} %dec_kv_ref.1, bf16[576,1024]{1,0:T(8,128)(2,1)} %bitcast.4, s32[16]{0:T(128)} %fill_ref.1, ...), custom_call_target="tpu_custom_call" | custom-call | flops 22817013760 | bytes 8388608 | tf_op jit(solution)/shard_map/pallas_call | solution.py:496
  72.2 2.2 %shard_map.131 = (bf16[64,1024]{1,0:T(8,128)(2,1)}, bf16[16,1024]{1,0:T(8,128)(2,1)}, bf16[576,1024]{1,0:T(8,128)(2,1)}) custom-call(bf16[80,1024]{1,0:T(8,128)(2,1)} %get-tuple-element.8.out_ref, bf16[576,1024]{1,0:T(8,128)(2,1)} %get-tuple-element.9.cache_ref), custom_call_target="tpu_custom_call" | custom-call | bytes 3145728 | tf_op jit(solution)/shard_map/pallas_call | solution.py:549

commit v5 on v4

--- a/solution.py
+++ b/solution.py
@@ -34,8 +34,8 @@
 
 PIECES = ((0, 0), (0, 1), (1, 0), (3, 1), (1, 1), (3, 0), (2, 0), (2, 1))
 HALF = POS // 2
-ORDER_BAND = (0, 1, 0, 1, 2, 7, 2, 7, 3, 6, 3, 6, 4, 5, 4, 5) + (4, 5, 3, 6, 2, 7) * 2 + (0, 1) * 2
-ORDER_KEYS = (0, 0, 1, 1) * 4 + (2,) * 6 + (3,) * 6 + (2, 2, 3, 3)
+ORDER_BAND = (0, 1, 2, 7, 0, 1, 2, 7, 3, 6, 3, 6, 4, 5, 4, 5) + (4, 5, 3, 6, 2, 7) * 2 + (0, 1) * 2
+ORDER_KEYS = (0, 0, 0, 0, 1, 1, 1, 1) + (0, 0, 1, 1) * 2 + (2,) * 6 + (3,) * 6 + (2, 2, 3, 3)
 STEPS = len(ORDER_BAND)
 FINISH = 22
 
@@ -67,10 +67,10 @@
 
 
 def kernel(
-    query_ref, dec_query_ref, span_kv_ref, dec_kv_ref, cache_ref, fill_ref, owner_ref, slot_ref, dlen_ref,
+    query_hbm, dec_query_hbm, span_kv_hbm, dec_kv_hbm, cache_ref, fill_ref, owner_ref, slot_ref, dlen_ref,
     uk_hbm, uv_hbm,
     out_ref, newc_hbm,
-    rows8, kv8, a_out, a_in, kv_out, kv_in, q_all, qr_all, k_all, k_own, uk, uv, newc,
+    query_ref, dec_query_ref, span_kv_ref, dec_kv_ref, q_in, dq_in, kv_in, dkv_in, q_rows, kv_rows32, q_all, qr_all, k_all, k_own, uk, uv, newc,
     acc, peak, total, score_a, score_b, best_a, best_b, weights, o_send, e_send, o_recv, e_recv,
     local_sem, a_send, a_recv, c_send, c_recv, h_send, h_recv, p_send, p_recv,
 ):
@@ -102,6 +102,14 @@
             barrier, inc=1, device_id=(lax.rem(seq + d, SEQ), grp), device_id_type=MESH
         )
 
+    inputs = [
+        pltpu.make_async_copy(query_hbm, query_ref, local_sem.at[5]),
+        pltpu.make_async_copy(dec_query_hbm, dec_query_ref, local_sem.at[6]),
+        pltpu.make_async_copy(span_kv_hbm, span_kv_ref, local_sem.at[7]),
+        pltpu.make_async_copy(dec_kv_hbm, dec_kv_ref, local_sem.at[8]),
+    ]
+    for c in inputs:
+        c.start()
     own_keys = [
         pltpu.make_async_copy(
             cache_ref.at[:, pl.ds(h * HALF, HALF)], k_all.at[h, pl.ds(0, KEY)], local_sem.at[4 * h]
@@ -115,28 +123,26 @@
     own_uk.start()
     own_uv.start()
 
-    rows8[...] = jnp.zeros(rows8.shape, F32)
-    rows8[0:4, :] = query_ref[...].astype(F32)
-    rows8[4:5, :] = dec_query_ref[...].astype(F32)
-    kv8[...] = jnp.zeros(kv8.shape, F32)
-    kv8[0:4, 0:KEY] = span_kv_ref[...].astype(F32)
-    kv8[4:5, 0:KEY] = dec_kv_ref[...].astype(F32)
-    kv_out[...] = kv8[...].astype(BF16)
-    for s in range(SEQ):
-        a_out[s] = rows8[:, s * SLICE : (s + 1) * SLICE].astype(BF16)
-    a_in[seq] = a_out[seq]
-    kv_in[seq] = kv_out[...]
-
     pl.semaphore_wait(barrier, SEQ - 1)
 
+    def heads_of(ref, device):
+        return ref.at[:, pl.ds(pl.multiple_of(device * SLICE, 128), SLICE)]
+
+    for c in inputs:
+        c.wait()
     exchange, exchange_kv = [], []
     for d in range(1, SEQ):
         peer = lax.rem(seq + d, SEQ)
-        exchange.append(remote(a_out.at[peer], a_in.at[seq], a_send.at[d - 1], a_recv.at[d - 1], peer))
-        exchange_kv.append(
-            remote(kv_out, kv_in.at[seq], a_send.at[SEQ + d - 2], a_recv.at[SEQ + d - 2], peer)
+        moves = (
+            (heads_of(query_ref, peer), q_in, exchange),
+            (heads_of(dec_query_ref, peer), dq_in, exchange),
+            (span_kv_ref, kv_in, exchange_kv),
+            (dec_kv_ref, dkv_in, exchange_kv),
         )
-    for c in exchange:
+        for at, (src, dst, group) in enumerate(moves):
+            i = (SEQ - 1) * at + d - 1
+            group.append(remote(src, dst.at[seq], a_send.at[i], a_recv.at[i], peer))
+    for c in exchange[0::2] + exchange[1::2]:
         c.start()
 
     def ring(halves, send, recv, peer_of):
@@ -196,24 +202,28 @@
 
     for c in own_keys:
         c.wait()
-    for c in exchange_kv:
+    for c in exchange_kv[0::2] + exchange_kv[1::2]:
         c.start()
     start(cring[0], cring[1])
+    mine = pl.ds(pl.multiple_of(seq * SLICE, 128), SLICE)
+    q_in[seq] = query_ref[:, mine]
+    dq_in[seq] = dec_query_ref[:, mine]
+    kv_in[seq] = span_kv_ref[...]
+    dkv_in[seq] = dec_kv_ref[...]
     unpack_keys(0)
     peak[...] = jnp.full(peak.shape, LOW, F32)
     total[...] = jnp.zeros(total.shape, F32)
     acc[...] = jnp.zeros(acc.shape, F32)
     e_send[...] = jnp.zeros(e_send.shape, F32)
 
-    prow = lax.broadcasted_iota(jnp.int32, (COUNT, 128), 0)
-    pcol = lax.broadcasted_iota(jnp.int32, (COUNT, 128), 1)
-    place = jnp.where(prow < SPAN, 8 * (prow // 4) + lax.rem(prow, 4), 8 * (prow - SPAN) + 4)
-    order = jnp.where(pcol == place, 1.0, 0.0).astype(BF16)
     own_uk.wait()
     for c in exchange:
         c.wait_recv()
-    got = a_in[...].astype(F32).reshape(8 * SEQ, SLICE).astype(BF16)
-    got = dot(order, got)
+    fours = SPAN // SEQ
+    for device in range(SEQ):
+        q_rows[fours * device : fours * (device + 1), :] = q_in[device].astype(F32)
+        q_rows[SPAN + device : SPAN + device + 1, :] = dq_in[device].astype(F32)
+    got = q_rows[...]
     for p in range(HEADS // 2):
         at = 3 * 128 * p
         t0, t1, t2 = (got[:, at + 128 * i : at + 128 * (i + 1)] for i in range(3))
@@ -236,8 +246,11 @@
 
     for c in exchange_kv:
         c.wait_recv()
-    kv_rows = kv_in[...].astype(F32).reshape(8 * SEQ, WIDE).astype(BF16)
-    kv_rows = dot(order, kv_rows).astype(BF16)
+    kv_rows32[...] = jnp.zeros(kv_rows32.shape, F32)
+    for device in range(SEQ):
+        kv_rows32[fours * device : fours * (device + 1), 0:KEY] = kv_in[device].astype(F32)
+        kv_rows32[SPAN + device : SPAN + device + 1, 0:KEY] = dkv_in[device].astype(F32)
+    kv_rows = kv_rows32[...].astype(BF16)
     k_own[...] = jnp.zeros(k_own.shape, BF16)
     k_own[0:COUNT, 0:DC] = kv_rows[:, 0:DC]
     k_own[0:COUNT, DC:WIDE] = dot(kv_rows[:, DC:WIDE], doubled()).astype(BF16)
@@ -351,12 +364,12 @@
     put_cache.start()
 
     def event(g):
-        @pl.when(g == 2)
+        @pl.when(g == 4)
         def _():
             arrived(cring[0], cring[1])
             unpack_keys(1)
 
-        @pl.when(g == 4)
+        @pl.when(g == 2)
         def _():
             arrived(hring[0], hring[1])
             start(hring[4], hring[5])
@@ -496,15 +509,19 @@
     out, new_cache = pl.pallas_call(
         kernel,
         out_shape=(shape((COUNT, HEADS * DV), BF16), shape((KEY, POS), BF16)),
-        in_specs=[vmem, vmem, vmem, vmem, hbm, smem, vmem, vmem, smem, hbm, hbm],
+        in_specs=[hbm, hbm, hbm, hbm, hbm, smem, vmem, vmem, smem, hbm, hbm],
         out_specs=(vmem, hbm),
         scratch_shapes=[
-            pltpu.VMEM((8, SEQ * SLICE), F32),
-            pltpu.VMEM((8, WIDE), F32),
-            pltpu.VMEM((SEQ, 8, SLICE), BF16),
-            pltpu.VMEM((SEQ, 8, SLICE), BF16),
-            pltpu.VMEM((8, WIDE), BF16),
-            pltpu.VMEM((SEQ, 8, WIDE), BF16),
+            pltpu.VMEM(query.shape, BF16),
+            pltpu.VMEM(dec_query.shape, BF16),
+            pltpu.VMEM(span_kv.shape, BF16),
+            pltpu.VMEM(dec_kv.shape, BF16),
+            pltpu.VMEM((SEQ, SPAN // SEQ, SLICE), BF16),
+            pltpu.VMEM((SEQ, ROWS // SEQ, SLICE), BF16),
+            pltpu.VMEM((SEQ, SPAN // SEQ, KEY), BF16),
+            pltpu.VMEM((SEQ, ROWS // SEQ, KEY), BF16),
+            pltpu.VMEM((COUNT, SLICE), F32),
+            pltpu.VMEM((COUNT, WIDE), F32),
             pltpu.VMEM((2 * SIDE, BAND, WIDE), BF16),
             pltpu.VMEM((2 * SIDE, BAND // 2, 128), BF16),
             pltpu.VMEM((2 * SIDE, WIDE, HALF), BF16),
@@ -524,9 +541,9 @@
             pltpu.VMEM((6, 8, 128), F32),
             pltpu.VMEM((6, BAND, DC), BF16),
             pltpu.VMEM((6, 8, 128), F32),
-            dma((5,)),
-            dma((2 * (SEQ - 1),)),
-            dma((2 * (SEQ - 1),)),
+            dma((9,)),
+            dma((4 * (SEQ - 1),)),
+            dma((4 * (SEQ - 1),)),
             dma((6,)),
             dma((6,)),
             dma((12,)),

time: 74.6 us -> 71.3 us (0.956)
  Pallas kernels: 73.8 us -> 70.5 us
    pallas_call x1, Pallas kernels: 71.6 us -> 68.2 us  [body(): pl.pallas_call(kernel, out_shape=(shape((COUNT, HEADS * DV), BF16), shape...]
where the time goes in v5:
time: 71.3 us; the launch traced here: 71.1 us
  Pallas kernels  70.5 us (99%)
    pallas_call x1, Pallas kernels, body(): pl.pallas_call(kernel, out_shape=(shape((COUNT, HEADS * DV), BF16), shape...  68.2 us
    pallas_call x1, Pallas kernels, body(): pl.pallas_call(hand_over, out_shape=(shape((SPAN, HEADS * DV), BF16), sha...  2.22 us

profile of v5, /device:TPU:0, one launch (start us, length us, event | category | flops | bytes accessed | tf_op | source)
XLA Modules:
  0.0 71.1 jit_solution(7130024538097978095)
XLA Ops:
  0.6 68.2 %shard_map.130 = (bf16[80,1024]{1,0:T(8,128)(2,1)}, bf16[576,1024]{1,0:T(8,128)(2,1)}) custom-call(bf16[4,24576]{1,0:T(4,128)(2,1)} %query_hbm.1, bf16[1,24576]{1,0:T(2,128)(2,1)} %dec_query_hbm.1, bf16[4,576]{1,0:T(4,128)(2,1)} %span_kv_hbm.1, bf16[1,576]{1,0:T(2,128)(2,1)} %dec_kv_hbm.1, bf16[576,1024]{1,0:T(8,128)(2,1)} %bitcast.4, s32[16]{0:T(128)} %fill_ref.1, ...), custom_call_target="tpu_custom_call" | custom-call | flops 22817013760 | bytes 8388608 | tf_op jit(solution)/shard_map/pallas_call | solution.py:509
  68.9 2.2 %shard_map.131 = (bf16[64,1024]{1,0:T(8,128)(2,1)}, bf16[16,1024]{1,0:T(8,128)(2,1)}, bf16[576,1024]{1,0:T(8,128)(2,1)}) custom-call(bf16[80,1024]{1,0:T(8,128)(2,1)} %get-tuple-element.8.out_ref, bf16[576,1024]{1,0:T(8,128)(2,1)} %get-tuple-element.9.cache_ref), custom_call_target="tpu_custom_call" | custom-call | bytes 3145728 | tf_op jit(solution)/shard_map/pallas_call | solution.py:566

commit v6 on v5

--- a/solution.py
+++ b/solution.py
@@ -123,8 +123,6 @@
     own_uk.start()
     own_uv.start()
 
-    pl.semaphore_wait(barrier, SEQ - 1)
-
     def heads_of(ref, device):
         return ref.at[:, pl.ds(pl.multiple_of(device * SLICE, 128), SLICE)]
 
@@ -142,8 +140,6 @@
         for at, (src, dst, group) in enumerate(moves):
             i = (SEQ - 1) * at + d - 1
             group.append(remote(src, dst.at[seq], a_send.at[i], a_recv.at[i], peer))
-    for c in exchange[0::2] + exchange[1::2]:
-        c.start()
 
     def ring(halves, send, recv, peer_of):
         count = len(halves(0, 0))
@@ -202,9 +198,6 @@
 
     for c in own_keys:
         c.wait()
-    for c in exchange_kv[0::2] + exchange_kv[1::2]:
-        c.start()
-    start(cring[0], cring[1])
     mine = pl.ds(pl.multiple_of(seq * SLICE, 128), SLICE)
     q_in[seq] = query_ref[:, mine]
     dq_in[seq] = dec_query_ref[:, mine]
@@ -215,6 +208,13 @@
     total[...] = jnp.zeros(total.shape, F32)
     acc[...] = jnp.zeros(acc.shape, F32)
     e_send[...] = jnp.zeros(e_send.shape, F32)
+
+    pl.semaphore_wait(barrier, SEQ - 1)
+    for c in exchange[0::2] + exchange[1::2]:
+        c.start()
+    for c in exchange_kv[0::2] + exchange_kv[1::2]:
+        c.start()
+    start(cring[0], cring[1])
 
     own_uk.wait()
     for c in exchange:
@@ -477,18 +477,18 @@
 
 
 def hand_over(out_ref, cache_ref, span_ref, dec_ref, new_ref, out, cache, sem):
-    half = KEY // 2
+    piece = KEY // 4
     ins = [pltpu.make_async_copy(out_ref, out, sem.at[0])]
     outs = [
         [
-            pltpu.make_async_copy(out.at[pl.ds(0, SPAN)], span_ref, sem.at[3]),
-            pltpu.make_async_copy(out.at[pl.ds(SPAN, ROWS)], dec_ref, sem.at[4]),
+            pltpu.make_async_copy(out.at[pl.ds(0, SPAN)], span_ref, sem.at[5]),
+            pltpu.make_async_copy(out.at[pl.ds(SPAN, ROWS)], dec_ref, sem.at[6]),
         ]
     ]
-    for i in range(2):
-        rows = pl.ds(i * half, half)
+    for i in range(4):
+        rows = pl.ds(i * piece, piece)
         ins.append(pltpu.make_async_copy(cache_ref.at[rows], cache.at[rows], sem.at[1 + i]))
-        outs.append([pltpu.make_async_copy(cache.at[rows], new_ref.at[rows], sem.at[5 + i])])
+        outs.append([pltpu.make_async_copy(cache.at[rows], new_ref.at[rows], sem.at[7 + i])])
     for c in ins:
         c.start()
     for c, then in zip(ins, outs):
@@ -575,7 +575,7 @@
         scratch_shapes=[
             pltpu.VMEM((COUNT, HEADS * DV), BF16),
             pltpu.VMEM((KEY, POS), BF16),
-            dma((7,)),
+            dma((11,)),
         ],
         compiler_params=pltpu.CompilerParams(vmem_limit_bytes=60 * 2**20),
         cost_estimate=pl.CostEstimate(flops=0, bytes_accessed=3 * 2**20, transcendentals=0),

time: 71.3 us -> 71 us (level)
  no operation moved by 1% of the time
where the time goes in v6:
time: 71 us; the launch traced here: 70.8 us
  Pallas kernels  70.2 us (99%)
    pallas_call x1, Pallas kernels, body(): pl.pallas_call(kernel, out_shape=(shape((COUNT, HEADS * DV), BF16), shape...  68 us
    pallas_call x1, Pallas kernels, body(): pl.pallas_call(hand_over, out_shape=(shape((SPAN, HEADS * DV), BF16), sha...  2.15 us

profile of v6, /device:TPU:0, one launch (start us, length us, event | category | flops | bytes accessed | tf_op | source)
XLA Modules:
  0.0 70.8 jit_solution(2500077127892601508)
XLA Ops:
  0.6 68.0 %shard_map.130 = (bf16[80,1024]{1,0:T(8,128)(2,1)}, bf16[576,1024]{1,0:T(8,128)(2,1)}) custom-call(bf16[4,24576]{1,0:T(4,128)(2,1)} %query_hbm.1, bf16[1,24576]{1,0:T(2,128)(2,1)} %dec_query_hbm.1, bf16[4,576]{1,0:T(4,128)(2,1)} %span_kv_hbm.1, bf16[1,576]{1,0:T(2,128)(2,1)} %dec_kv_hbm.1, bf16[576,1024]{1,0:T(8,128)(2,1)} %bitcast.4, s32[16]{0:T(128)} %fill_ref.1, ...), custom_call_target="tpu_custom_call" | custom-call | flops 22817013760 | bytes 8388608 | tf_op jit(solution)/shard_map/pallas_call | solution.py:509
  68.7 2.2 %shard_map.131 = (bf16[64,1024]{1,0:T(8,128)(2,1)}, bf16[16,1024]{1,0:T(8,128)(2,1)}, bf16[576,1024]{1,0:T(8,128)(2,1)}) custom-call(bf16[80,1024]{1,0:T(8,128)(2,1)} %get-tuple-element.8.out_ref, bf16[576,1024]{1,0:T(8,128)(2,1)} %get-tuple-element.9.cache_ref), custom_call_target="tpu_custom_call" | custom-call | bytes 3145728 | tf_op jit(solution)/shard_map/pallas_call | solution.py:566

commit v7 on v6

--- a/solution.py
+++ b/solution.py
@@ -210,8 +210,10 @@
     e_send[...] = jnp.zeros(e_send.shape, F32)
 
     pl.semaphore_wait(barrier, SEQ - 1)
-    for c in exchange[0::2] + exchange[1::2]:
-        c.start()
+    far = sorted(range(1, SEQ), key=lambda d: -min(d // SIDE, SIDE - d // SIDE) - min(d % SIDE, SIDE - d % SIDE))
+    for first in range(2):
+        for d in far:
+            exchange[2 * (d - 1) + first].start()
     for c in exchange_kv[0::2] + exchange_kv[1::2]:
         c.start()
     start(cring[0], cring[1])

time: 71 us -> 71 us (level)
  no operation moved by 1% of the time
where the time goes in v7:
time: 71 us; the launch traced here: 70.9 us
  Pallas kernels  70.2 us (99%)
    pallas_call x1, Pallas kernels, body(): pl.pallas_call(kernel, out_shape=(shape((COUNT, HEADS * DV), BF16), shape...  68.1 us
    pallas_call x1, Pallas kernels, body(): pl.pallas_call(hand_over, out_shape=(shape((SPAN, HEADS * DV), BF16), sha...  2.15 us

profile of v7, /device:TPU:0, one launch (start us, length us, event | category | flops | bytes accessed | tf_op | source)
XLA Modules:
  0.0 70.9 jit_solution(14853236424948589713)
XLA Ops:
  0.6 68.1 %shard_map.130 = (bf16[80,1024]{1,0:T(8,128)(2,1)}, bf16[576,1024]{1,0:T(8,128)(2,1)}) custom-call(bf16[4,24576]{1,0:T(4,128)(2,1)} %query_hbm.1, bf16[1,24576]{1,0:T(2,128)(2,1)} %dec_query_hbm.1, bf16[4,576]{1,0:T(4,128)(2,1)} %span_kv_hbm.1, bf16[1,576]{1,0:T(2,128)(2,1)} %dec_kv_hbm.1, bf16[576,1024]{1,0:T(8,128)(2,1)} %bitcast.4, s32[16]{0:T(128)} %fill_ref.1, ...), custom_call_target="tpu_custom_call" | custom-call | flops 22817013760 | bytes 8388608 | tf_op jit(solution)/shard_map/pallas_call | solution.py:511
  68.7 2.2 %shard_map.131 = (bf16[64,1024]{1,0:T(8,128)(2,1)}, bf16[16,1024]{1,0:T(8,128)(2,1)}, bf16[576,1024]{1,0:T(8,128)(2,1)}) custom-call(bf16[80,1024]{1,0:T(8,128)(2,1)} %get-tuple-element.8.out_ref, bf16[576,1024]{1,0:T(8,128)(2,1)} %get-tuple-element.9.cache_ref), custom_call_target="tpu_custom_call" | custom-call | bytes 3145728 | tf_op jit(solution)/shard_map/pallas_call | solution.py:568
